TPU v7x, 256 devices: a whole 4x4x8 slice. The times are simulated.
256 devices in a mesh: seq: 64 (over z, x, core), head: 4 (over y).
Axes of the slice: x: 4, y: 4, z: 8, core: 2. Of those that a mesh axis runs over, the one named last changes fastest.
Arguments:
- query_vectors: bfloat16 [8192, 4096], P('seq', 'head'), may hold values from -6 to 6
- key_vectors: bfloat16 [8192, 4096], P('seq', 'head'), may hold values from -6 to 6
- value_vectors: bfloat16 [8192, 4096], P('seq', 'head'), may hold values from -6 to 6
- log_decay: float32 [32, 8192], P('head', 'seq'), may hold values from -1.5 to 0, as said below
- write_strength: float32 [32, 8192], P('head', 'seq'), may hold values from 0 to 1, as said below
- output_gate: bfloat16 [8192, 4096], P('seq', 'head'), may hold values from -6 to 6
- norm_gain: float32 [128], replicated, may hold values from 0.1 to 1.9
- out_proj: bfloat16 [4096, 2304], P('head'), may hold values from -0.09375 to 0.09375
Outputs:
- mixed: bfloat16 [8192, 2304], P(('seq', 'head'))
Inputs may be any that keep to these rules, and one draw needn't show every extreme that they name: `log_decay`: every entry is at most zero. `write_strength`: every entry is positive.
All inputs are finite; a program needn't handle non-finite values.
Results may differ from a plain program's by a relative error of at most 0.015.
Values may be sent and summed in bfloat16 or wider, within the bound.
A program may use at most 192 MiB of HBM per device.

v0:
```python
import jax
import jax.numpy as jnp
from jax import lax
from jax.sharding import PartitionSpec as P

GROUP = 64


HIGH = lax.Precision.HIGHEST


def prefix(part, axis, combine, identity):
    place = lax.axis_index(axis)
    gathered = jax.tree.map(lambda a: lax.all_gather(a, axis), part)
    state = jax.tree.map(lambda a, e: jnp.zeros_like(a) + jnp.asarray(e, a.dtype), part, identity)

    def one(lap, state):
        return combine(
            state, jax.tree.map(lambda a: lax.dynamic_index_in_dim(a, lap, 0, False), gathered)
        )

    return lax.fori_loop(0, place, one, state)


def dot_high(left, right):
    return jnp.dot(left, right, precision=HIGH, preferred_element_type=jnp.float32)


def group_terms(query, keyrow, value, decay, strength):
    width = keyrow.shape[1]
    vwidth = value.shape[1]
    length = keyrow.shape[0]
    query = query * lax.rsqrt(jnp.sum(query * query, axis=1, keepdims=True) + 1e-06)
    keyrow = keyrow * lax.rsqrt(jnp.sum(keyrow * keyrow, axis=1, keepdims=True) + 1e-06)
    cumul = jnp.cumsum(decay)
    spread = cumul[:, None] - cumul[None, :]
    places = jnp.arange(length)
    lower = places[:, None] >= places[None, :]
    strict = places[:, None] > places[None, :]
    ratio = jnp.where(lower, jnp.exp(jnp.minimum(spread, 0.0)), 0.0)
    couple = strength[:, None] * jnp.where(strict, ratio, 0.0) * dot_high(keyrow, keyrow.T)
    growth = jnp.exp(cumul)
    rhs = strength[:, None] * jnp.concatenate([value, growth[:, None] * keyrow], axis=1)
    solved = jax.scipy.linalg.solve_triangular(
        jnp.eye(length, dtype=jnp.float32) + couple, rhs, lower=True, unit_diagonal=True
    )
    score_values = ratio * dot_high(query, keyrow.T)
    both = dot_high(score_values, solved)
    tail = jnp.exp(cumul[-1] - cumul)
    ends = dot_high((tail[:, None] * keyrow).T, solved)
    transit = growth[-1] * jnp.eye(width, dtype=jnp.float32) - ends[:, vwidth:]
    inject = ends[:, :vwidth]
    reach = growth[:, None] * query - both[:, vwidth:]
    local = both[:, :vwidth]
    return (transit, inject, reach, local)


def apply_heads(square_array, state):
    return jnp.einsum("hij,hjk->hik", square_array, state, precision=HIGH)


def compose(earlier, later):
    power_early, state_early = earlier
    power_late, memory_final = later
    return (
        apply_heads(power_late, power_early),
        apply_heads(power_late, state_early) + memory_final,
    )


def on_device(
    query_vectors,
    key_vectors,
    value_vectors,
    log_decay,
    write_strength,
    output_gate,
    norm_gain,
    out_proj,
):
    rows = query_vectors.shape[0]
    heads = log_decay.shape[0]
    width = query_vectors.shape[1] // heads
    vwidth = value_vectors.shape[1] // heads
    blocks = rows // GROUP

    def split_heads(array, size):
        return array.reshape(blocks, GROUP, heads, size).transpose(2, 0, 1, 3).astype(jnp.float32)

    terms = jax.vmap(jax.vmap(group_terms), in_axes=1, out_axes=0)(
        split_heads(query_vectors, width),
        split_heads(key_vectors, width),
        split_heads(value_vectors, vwidth),
        log_decay.reshape(heads, blocks, GROUP),
        write_strength.reshape(heads, blocks, GROUP),
    )
    transit, inject, reach, local = terms
    identity = jnp.broadcast_to(jnp.eye(width, dtype=jnp.float32), (heads, width, width))
    empty = jnp.zeros((heads, width, vwidth), jnp.float32)

    def fold_block(carry, item):
        power, state = carry
        tr_mat, input_matrix = item
        return ((apply_heads(tr_mat, power), apply_heads(tr_mat, state) + input_matrix), None)

    (total_power, total_state), _ = lax.scan(fold_block, (identity, empty), (transit, inject))
    _, incoming = prefix((total_power, total_state), "seq", compose, (identity, empty))

    def rerun_block(state, item):
        tr_mat, input_matrix, re_mat, lo_mat = item
        output = apply_heads(re_mat, state) + lo_mat
        return (apply_heads(tr_mat, state) + input_matrix, output)

    _, outputs = lax.scan(rerun_block, incoming, (transit, inject, reach, local))
    outputs = outputs.transpose(0, 2, 1, 3).reshape(rows, heads, vwidth)
    square = jnp.mean(outputs * outputs, axis=2, keepdims=True)
    gating = jax.nn.sigmoid(output_gate.reshape(rows, heads, vwidth).astype(jnp.float32))
    rescaled_heads = (
        (outputs * lax.rsqrt(square + 1e-06) * norm_gain * gating)
        .astype(jnp.bfloat16)
        .reshape(rows, heads * vwidth)
    )
    return lax.psum_scatter(
        jnp.dot(rescaled_heads, out_proj, preferred_element_type=jnp.float32).astype(jnp.bfloat16),
        "head",
        scatter_dimension=0,
        tiled=True,
    )


def solution(mesh):
    in_specs = (
        P("seq", "head"),
        P("seq", "head"),
        P("seq", "head"),
        P("head", "seq"),
        P("head", "seq"),
        P("seq", "head"),
        P(),
        P("head", None),
    )
    out_specs = P(("seq", "head"), None)
    return jax.shard_map(
        on_device, mesh=mesh, in_specs=in_specs, out_specs=out_specs, check_vma=False
    )
```

profile of v0, /device:TPU:224, one launch (start us, length us, event | category | flops | bytes accessed | tf_op | source)
XLA Modules:
  0.0 548.9 jit_solution(12087305418464698067)
XLA Ops:
  14.4 78.6 %custom-call.4 = f32[2,8,1,64,64]{3,4,2,1,0:T(8,128)S(1)} custom-call(f32[2,8,1,64,64]{4,3,2,1,0:T(8,128)S(1)} %fusion.25), custom_call_target="InvertDiagBlocksLowerTriangular" | custom-call | tf_op jit(solution)/shard_map/vmap(vmap(jit(_solve_triangular)))/triangular_solve | solution.py:44
  94.7 2.3 fusion.36
  97.2 2.9 while.39
  101.9 2.2 convolution_multiply_fusion
  104.1 2.2 fusion.54
  107.5 134.5 %all-gather.7.cloned.1.call-done = f32[512,128,128]{2,1,0:T(8,128)} async-done(((f32[8,128,128]{2,1,0:T(8,128)}), f32[512,128,128]{2,1,0:T(8,128)}) %all-gather.7.cloned.1.call-update) | async-done | bytes 33554448 | tf_op jit(solution)/shard_map/all_gather | solution.py:14
  242.1 142.3 %all-gather.5.cloned.1.call-done = f32[512,128,128]{2,1,0:T(8,128)} async-done(((f32[8,128,128]{2,1,0:T(8,128)}), f32[512,128,128]{2,1,0:T(8,128)}) %all-gather.5.cloned.1.call-update) | async-done | bytes 33554448 | tf_op jit(solution)/shard_map/all_gather | solution.py:14
  384.4 110.0 %while.37 = (s32[]{:T(128)}, f32[8,128,128]{2,1,0:T(8,128)S(1)}, s32[]{:T(128)}, f32[64,8,128,128]{3,2,1,0:T(8,128)}, f32[64,8,128,128]{3,2,1,0:T(8,128)}, /*index=5*/s32[]{:T(128)}, s32[]{:T(128)}, s32[]{:T(128)}) while((s32[]{:T(128)}, f32[8,128,128]{2,1,0:T(8,128)S(1)}, s32[]{:T(128)}, f32[64,8,128,128]{3,2,1,0:T(8,128)}, ...), condition=%wide.region_5.6_spmd, body=%wide.region_4.5_spmd.sunk | while | flops 201457664 | bytes 3146879 | solution.py:22
  384.6 1.9 convolution_add_fusion.7
  386.6 1.9 convolution_add_fusion.7
  388.5 1.9 convolution_add_fusion.7
  390.5 1.9 convolution_add_fusion.7
  392.5 1.9 convolution_add_fusion.7
  394.4 1.9 convolution_add_fusion.7
  396.4 1.9 convolution_add_fusion.7
  400.3 1.9 convolution_add_fusion.7
  402.3 1.9 convolution_add_fusion.7
  404.2 1.9 convolution_add_fusion.7
  406.2 1.9 convolution_add_fusion.7
  408.2 1.9 convolution_add_fusion.7
  410.1 1.9 convolution_add_fusion.7
  421.9 1.9 convolution_add_fusion.7
  423.8 1.9 convolution_add_fusion.7
  425.8 1.9 convolution_add_fusion.7
  427.8 1.9 convolution_add_fusion.7
  429.7 1.9 convolution_add_fusion.7
  431.7 1.9 convolution_add_fusion.7
  443.5 1.9 convolution_add_fusion.7
  445.4 1.9 convolution_add_fusion.7
  447.4 1.9 convolution_add_fusion.7
  449.3 1.9 convolution_add_fusion.7
  451.3 1.9 convolution_add_fusion.7
  453.3 1.9 convolution_add_fusion.7
  465.0 1.9 convolution_add_fusion.7
  467.0 1.9 convolution_add_fusion.7
  469.0 1.9 convolution_add_fusion.7
  470.9 1.9 convolution_add_fusion.7
  472.9 1.9 convolution_add_fusion.7
  474.8 1.9 convolution_add_fusion.7
  486.6 1.9 convolution_add_fusion.7
  488.6 1.9 convolution_add_fusion.7
  490.5 1.9 convolution_add_fusion.7
  492.5 1.9 convolution_add_fusion.7
  494.4 6.0 %while.38 = (s32[]{:T(128)}, f32[8,128,128]{2,1,0:T(8,128)S(1)}, f32[2,8,64,128]{3,2,1,0:T(8,128)}, f32[2,8,128,128]{3,2,1,0:T(8,128)S(1)}, f32[2,8,128,128]{3,2...) while((s32[]{:T(128)}, f32[8,128,128]{2,1,0:T(8,128)S(1)}, ...), condition=%wide.region_8.9_spmd, body=%wide.region_7.8_spmd.sunk | while | flops 302186496 | bytes 4458589 | solution.py:114
  494.5 2.3 fusion.81
  497.5 2.3 fusion.81
  503.4 4.1 convolution_convert_fusion
  507.6 34.8 %reduce-scatter.2.cloned.1.call-done = bf16[32,2304]{1,0:T(8,128)(2,1)} async-done(((bf16[128,2304]{1,0:T(8,128)(2,1)}), bf16[32,2304]{1,0:T(8,128)(2,1)}) %reduce-scatter.2.cloned.1.call-update) | async-done | bytes 147472 | tf_op jit(solution)/shard_map/reduce_scatter | solution.py:123
  (154 shorter events, 61.3 us)
Async XLA Ops:
  6.5 95.4 %copy-start = (f32[128]{0:T(128)S(1)}, f32[128]{0:T(128)}, u32[]{:S(2)}) copy-start(f32[128]{0:T(128)} %param.20) | copy-start | bytes 1540
  6.5 5.6 %copy-start.6 = (bf16[128,1024]{1,0:T(8,128)(2,1)S(1)}, bf16[128,1024]{1,0:T(8,128)(2,1)}, u32[]{:S(2)}) copy-start(bf16[128,1024]{1,0:T(8,128)(2,1)} %param.14) | copy-start | bytes 786436
  6.5 235.5 %all-gather.7.cloned.1.call-start = ((), (), s32[]{:S(2)}) async-start(), calls=%async_computation.3 | async-start | bytes 34078720 | tf_op jit(solution)/shard_map/all_gather | solution.py:14
  13.1 83.8 %copy-start.5 = (f32[16,8,8,128]{3,2,1,0:T(8,128)}, f32[16,8,8,128]{3,2,1,0:T(8,128)S(1)}, u32[]{:S(2)}) copy-start(f32[16,8,8,128]{3,2,1,0:T(8,128)S(1)} %copy.50) | copy-start | bytes 1572868
  94.6 2.3 copy-start.4
  100.1 0.8 copy-start.3
  100.1 1.0 copy-start.2
  100.9 283.4 %all-gather.5.cloned.1.call-start = ((), (), s32[]{:S(2)}) async-start(), calls=%async_computation.2 | async-start | bytes 34078720 | tf_op jit(solution)/shard_map/all_gather | solution.py:14
  101.7 440.7 %reduce-scatter.2.cloned.1.call-start = ((), (), s32[]{:S(2)}) async-start(), calls=%async_computation.1 | async-start | bytes 737280 | tf_op jit(solution)/shard_map/reduce_scatter | solution.py:123
  494.4 9.0 %copy-start.7 = (bf16[128,1024]{1,0:T(8,128)(2,1)S(1)}, bf16[128,1024]{1,0:T(8,128)(2,1)}, u32[]{:S(2)}) copy-start(bf16[128,1024]{1,0:T(8,128)(2,1)} %param.19) | copy-start | bytes 786436
  501.8 40.5 %copy-start.1 = (f32[128]{0:T(128)S(1)}, f32[128]{0:T(128)}, u32[]{:S(2)}) copy-start(f32[128]{0:T(128)} %param.20) | copy-start | bytes 1540
Sparse Core Ops, SparseCore 0:
  101.1 140.9 all-gather.6
  244.8 139.4 all-gather.4
  507.7 34.6 reduce-scatter.1
where the time goes:
time: 553 us; the launch traced here: 549 us
  waiting for transfers between devices  312 us (56%)
  matrix products  128 us (23%)
  other arithmetic  85.8 us (16%)
  between operations  13.5 us (2%)
  local copies, waits for them, and re-layouts  7.31 us (1%)
    all_gather x2, waiting for transfers between devices, prefix(): gathered = jax.tree.map(lambda a: lax.all_gather(a, axis), part)  277 us
    dot_general x64, matrix products, apply_heads(): return jnp.einsum('hij,hjk->hik', square_array, state, precision=HIGH)  114 us
    another operation x4, other arithmetic, group_terms(): jax.scipy.linalg.solve_triangular(jnp.eye(length, dtype=jnp.float32) + co...  78.7 us
    reduce_scatter x1, waiting for transfers between devices, on_device(): lax.psum_scatter(jnp.dot(rescaled_heads, out_proj, preferred_element_type...  34.8 us
  transfers between devices with their start and end apart: 3, of which 3 were waited for; matrix products, arithmetic and copies ran while one was open for 1% of the time, Pallas kernels for 0%

commit v1 on v0

v1 whole, which is shorter than its diff:
```python
import jax
import jax.numpy as jnp
from jax import lax
from jax.experimental import pallas as pl
from jax.experimental.pallas import tpu as pltpu
from jax.sharding import PartitionSpec as P

MESH = pl.DeviceIdType.MESH
F32 = jnp.float32
BF16 = jnp.bfloat16

ROW = 8
DEEP = 8
FANS = 4
HEADS = 8
N = 128
GROWS = 16
MSG = GROWS + 2 * N
CHUNKS = 3
EPS = 1e-06


def bdot(left, right, dims):
    return lax.dot_general(
        left.astype(BF16), right.astype(BF16), (dims, ((0,), (0,))), preferred_element_type=F32
    )


NN = ((2,), (1,))
NT = ((2,), (2,))
TN = ((1,), (1,))


def split(x):
    high = x.astype(BF16)
    return high, (x - high.astype(F32)).astype(BF16)


def bdot_left(left, right, dims=NN):
    high, low = split(left)
    return bdot(high, right, dims) + bdot(low, right, dims)


def bdot_right(left, right, dims=NN):
    high, low = split(right)
    return bdot(left, high, dims) + bdot(left, low, dims)


def bdot_both(left, right, dims=NN):
    lh, ll = split(left)
    rh, rl = split(right)
    return bdot(lh, rh, dims) + (bdot(lh, rl, dims) + bdot(ll, rh, dims))


def dot(left, right):
    return jnp.dot(left.astype(BF16), right.astype(BF16), preferred_element_type=F32)


def dot_left(left, right):
    high, low = split(left)
    return dot(high, right) + dot(low, right)


def inverse(couple, row, col):
    def level(size):
        pair = (row // (2 * size)) == (col // (2 * size))
        return pair & ((row // size) % 2 == 1) & ((col // size) % 2 == 0)

    eye = jnp.where(row == col, 1.0, 0.0).astype(F32)
    solved = eye - jnp.where(level(1), couple, 0.0)
    size = 2
    while size < N:
        below = jnp.where(level(size), couple, 0.0)
        solved = solved - bdot(solved, bdot(below, solved, NN), NN)
        size *= 2
    rest = (eye - solved) - bdot_both(couple, solved)
    return solved + bdot(solved, rest, NN)


def local_terms(query, keyrow, value, cum_row, cum_col, str_row, str_col):
    shape = query.shape
    row = lax.broadcasted_iota(jnp.int32, shape, 1)
    col = lax.broadcasted_iota(jnp.int32, shape, 2)
    keykey = bdot(keyrow, keyrow, NT)
    diag = jnp.where(row == col, keykey, 0.0)
    kscale_row = lax.rsqrt(jnp.sum(diag, axis=1, keepdims=True) + EPS)
    kscale_col = lax.rsqrt(jnp.sum(diag, axis=2, keepdims=True) + EPS)
    ratio = jnp.where(row >= col, jnp.exp(jnp.minimum(cum_col - cum_row, 0.0)), 0.0) * kscale_row
    couple = jnp.where(row > col, ratio * keykey, 0.0) * (str_col * kscale_col)
    solved = inverse(couple, row, col)
    from_value = bdot_left(solved * str_row, value)
    from_key = bdot_left(solved * (str_row * jnp.exp(cum_row) * kscale_row), keyrow)
    both = jnp.concatenate([from_key, from_value], axis=2)
    last = cum_row[:, :, N - 1 :]
    tail = jnp.exp(last - cum_col) * kscale_col
    ends = bdot_right(keyrow, both * tail, TN)
    return ratio, both, ends, jnp.exp(last)


def local_reads(query, keyrow, ratio, both, cum_col):
    query32 = query.astype(F32)
    qscale = lax.rsqrt(jnp.sum(query32 * query32, axis=2, keepdims=True) + EPS)
    score = ratio * bdot(query, keyrow, NT) * qscale
    read = bdot_both(score, both)
    reach = query32 * (jnp.exp(cum_col) * qscale) - read[:, :, :N]
    return reach, read[:, :, N:]


def decay_rows(gain):
    place = lax.broadcasted_iota(jnp.int32, (GROWS, N), 0)
    high = gain.astype(BF16).astype(F32)
    middle = (gain - high).astype(BF16).astype(F32)
    low = gain - high - middle
    rows = jnp.where(place == 0, high, jnp.where(place == 1, middle, jnp.where(place == 2, low, 0.0)))
    return rows.astype(BF16)


def read_message(buffer, index):
    gain = jnp.sum(buffer[index, :GROWS, :].astype(F32), axis=0, keepdims=True)
    return gain, buffer[index, GROWS : GROWS + N, :], buffer[index, GROWS + N :, :]


def kernel(
    q_ref,
    k_ref,
    v_ref,
    decay_ref,
    strength_ref,
    gain_ref,
    gate_any,
    proj_any,
    out_ref,
    gate_buf,
    proj_buf,
    head_send,
    head_recv,
    pre_d,
    pre_j,
    pre_g,
    total_buf,
    state_send,
    state_recv,
    reach_buf,
    local_buf,
    normed_buf,
    part_buf,
    part_recv,
    load_sem,
    hs_sem,
    hr_sem,
    rs_sem,
    rr_sem,
    ls_sem,
    lr_sem,
    ss_sem,
    sr_sem,
    ps_sem,
    pr_sem,
):
    place = lax.axis_index("seq")
    fan = lax.axis_index("head")
    deep = place // ROW
    mine = lax.rem(place, ROW)
    right = lax.rem(deep + 1, DEEP)
    left = lax.rem(deep + DEEP - 1, DEEP)
    row_peers = [lax.rem(mine + step, ROW) for step in range(1, ROW)]
    fan_peers = [lax.rem(fan + step, FANS) for step in (2, 1, 3)]

    loads = [
        pltpu.make_async_copy(gate_any, gate_buf, load_sem.at[0]),
        pltpu.make_async_copy(proj_any, proj_buf, load_sem.at[1]),
    ]
    for load in loads:
        load.start()

    barrier = pltpu.get_barrier_semaphore()
    greeted = [(deep * ROW + peer, fan) for peer in row_peers]
    greeted += [(right * ROW + mine, fan), (left * ROW + mine, fan)]
    greeted += [(place, peer) for peer in fan_peers]
    for device in greeted:
        pl.semaphore_signal(barrier, inc=1, device_id=device, device_id_type=MESH)

    def remote(source, target, send, recv, device):
        return pltpu.make_async_remote_copy(
            src_ref=source,
            dst_ref=target,
            send_sem=send,
            recv_sem=recv,
            device_id=device,
            device_id_type=MESH,
        )

    tri_row = lax.broadcasted_iota(jnp.int32, (N, N), 0)
    tri_col = lax.broadcasted_iota(jnp.int32, (N, N), 1)
    upper = jnp.where(tri_row <= tri_col, 1.0, 0.0).astype(F32)
    strength = strength_ref[...]
    cumul = jnp.dot(
        decay_ref[...], upper, precision=lax.Precision.HIGHEST, preferred_element_type=F32
    )
    turned = jnp.concatenate([cumul, strength, jnp.zeros((N - 2 * HEADS, N), F32)], axis=0).T
    heads = range(HEADS)
    cum_row = jnp.stack([cumul[h : h + 1, :] for h in heads])
    str_row = jnp.stack([strength[h : h + 1, :] for h in heads])
    cum_col = jnp.stack([turned[:, h : h + 1] for h in heads])
    str_col = jnp.stack([turned[:, HEADS + h : HEADS + h + 1] for h in heads])
    query, keyrow, value = (
        jnp.stack([ref[:, h * N : (h + 1) * N] for h in heads]) for ref in (q_ref, k_ref, v_ref)
    )
    ratio, both, ends, last = local_terms(
        query, keyrow, value, cum_row, cum_col, str_row, str_col
    )
    head_send[:, GROWS : GROWS + N, :] = (-ends[:, :, :N]).astype(BF16)
    head_send[:, GROWS + N :, :] = ends[:, :, N:].astype(BF16)
    for h in heads:
        head_send[h, :GROWS, :] = decay_rows(jnp.broadcast_to(last[h], (GROWS, N)))

    pl.semaphore_wait(barrier, len(greeted))
    head_copies = [
        remote(
            head_send.at[peer],
            head_recv.at[mine],
            hs_sem.at[peer],
            hr_sem.at[mine],
            (deep * ROW + peer, fan),
        )
        for peer in row_peers
    ]
    for copy in head_copies:
        copy.start()
    head_recv[mine] = head_send[mine]

    reach, local = local_reads(query, keyrow, ratio, both, cum_col)
    reach_buf[...] = reach
    local_buf[...] = local

    for i in range(ROW):

        @pl.when(mine != i)
        def _():
            remote(
                head_send.at[i], head_recv.at[i], hs_sem.at[i], hr_sem.at[i], (deep * ROW + i, fan)
            ).wait_recv()

    gains = jnp.ones((1, N), F32)
    run_d = jnp.zeros((N, N), F32)
    run_j = jnp.zeros((N, N), F32)
    for i in range(ROW):
        pre_g[i] = jnp.broadcast_to(gains, (8, N))
        pre_d[pl.ds(i * N, N), :] = run_d.astype(BF16)
        pre_j[i] = run_j
        gain, step_d, step_j = read_message(head_recv, i)
        if i == 0:
            run_d, run_j = step_d.astype(F32), step_j.astype(F32)
        else:
            high, low = split(jnp.concatenate([run_d, run_j], axis=1))
            prod = dot(step_d, high) + dot(step_d, low)
            run_d = gain * run_d + gains * step_d.astype(F32) + prod[:, :N]
            run_j = gain * run_j + step_j.astype(F32) + prod[:, N:]
        gains = gains * gain
    total_buf[deep, :GROWS, :] = decay_rows(jnp.broadcast_to(gains, (GROWS, N)))
    total_buf[deep, GROWS : GROWS + N, :] = run_d.astype(BF16)
    total_buf[deep, GROWS + N :, :] = run_j.astype(BF16)

    half = DEEP // 2

    def ring(step, sign, send, recv):
        slot = lax.rem(deep + DEEP - sign * (step - 1), DEEP)
        to = right if sign > 0 else left
        return remote(
            total_buf.at[slot],
            total_buf.at[slot],
            send.at[step - 1],
            recv.at[step - 1],
            (to * ROW + mine, fan),
        )

    def arrived(step, sign, send, recv):
        slot = lax.rem(deep + DEEP - sign * step, DEEP)
        remote(
            total_buf.at[slot],
            total_buf.at[slot],
            send.at[step - 1],
            recv.at[step - 1],
            ((left if sign > 0 else right) * ROW + mine, fan),
        ).wait_recv()
        return slot

    rings = [ring(1, 1, rs_sem, rr_sem), ring(1, -1, ls_sem, lr_sem)]
    for copy in rings:
        copy.start()
    near_g = jnp.ones((1, N), F32)
    near_d = jnp.zeros((N, N), F32)
    near_j = jnp.zeros((N, N), F32)
    far = jnp.zeros((N, N), F32)
    for step in range(1, half + 1):
        slot = arrived(step, 1, rs_sem, rr_sem)
        if step < half:
            copy = ring(step + 1, 1, rs_sem, rr_sem)
            copy.start()
            rings.append(copy)
        if step < half:
            far_slot = arrived(step, -1, ls_sem, lr_sem)
            if step < half - 1:
                copy = ring(step + 1, -1, ls_sem, lr_sem)
                copy.start()
                rings.append(copy)
        gain, step_d, step_j = read_message(total_buf, slot)
        valid = deep >= step
        gain = jnp.where(valid, gain, 1.0)
        step_d = jnp.where(valid, step_d.astype(F32), 0.0)
        step_j = jnp.where(valid, step_j.astype(F32), 0.0)
        prod = dot_left(near_d, jnp.concatenate([step_d, step_j], axis=1))
        near_j = near_j + near_g * step_j + prod[:, N:]
        near_d = near_g * step_d + gain * near_d + prod[:, :N]
        near_g = near_g * gain
        if step < half:
            gain, step_d, step_j = read_message(total_buf, far_slot)
            high, low = split(far)
            moved = gain * far + dot(step_d, high) + dot(step_d, low) + step_j.astype(F32)
            far = jnp.where(deep + step >= DEEP, moved, far)
    state = near_g * far + dot_left(near_d, far) + near_j

    starts = dot(pre_d[...], state)
    for i in range(ROW):
        first = pre_g[i, :1, :] * state + starts[i * N : (i + 1) * N] + pre_j[i]
        state_send[i] = first.astype(BF16)
    state_copies = [
        remote(
            state_send.at[peer],
            state_recv.at[mine],
            ss_sem.at[peer],
            sr_sem.at[mine],
            (deep * ROW + peer, fan),
        )
        for peer in row_peers
    ]
    for copy in state_copies:
        copy.start()
    state_recv[mine] = state_send[mine]
    loads[0].wait()
    gating = jax.nn.sigmoid(gate_buf[...].astype(F32)) * jnp.tile(gain_ref[...], (1, HEADS))
    for peer in row_peers:
        remote(
            state_send.at[peer],
            state_recv.at[peer],
            ss_sem.at[peer],
            sr_sem.at[peer],
            (deep * ROW + peer, fan),
        ).wait_recv()
    outputs = bdot_left(reach_buf[...], state_recv[...]) + local_buf[...]
    square = jnp.mean(outputs * outputs, axis=2, keepdims=True)
    outputs = outputs * lax.rsqrt(square + EPS)
    for h in heads:
        columns = slice(h * N, (h + 1) * N)
        normed_buf[:, columns] = (outputs[h] * gating[:, columns]).astype(BF16)

    loads[1].wait()
    rows = N // FANS
    width = proj_buf.shape[1] // CHUNKS
    part_copies = []
    for c in range(CHUNKS):
        part_buf[c] = jnp.dot(
            normed_buf[...],
            proj_buf[:, c * width : (c + 1) * width],
            preferred_element_type=F32,
        ).astype(BF16)
        for n, peer in enumerate(fan_peers):
            copy = remote(
                part_buf.at[c, pl.ds(pl.multiple_of(peer * rows, rows), rows), :],
                part_recv.at[c, fan],
                ps_sem.at[c, n],
                pr_sem.at[c, fan],
                (place, peer),
            )
            copy.start()
            part_copies.append(copy)
        part_recv[c, fan] = part_buf[c, pl.ds(pl.multiple_of(fan * rows, rows), rows), :]
    for c in range(CHUNKS):
        for n, peer in enumerate(fan_peers):
            remote(
                part_buf.at[c, pl.ds(pl.multiple_of(peer * rows, rows), rows), :],
                part_recv.at[c, peer],
                ps_sem.at[c, n],
                pr_sem.at[c, peer],
                (place, peer),
            ).wait_recv()
        summed = part_recv[c, 0].astype(F32)
        for n in range(1, FANS):
            summed = summed + part_recv[c, n].astype(F32)
        out_ref[:, c * width : (c + 1) * width] = summed.astype(BF16)

    for copy in head_copies + rings + state_copies + part_copies:
        copy.wait_send()


def on_device(
    query_vectors,
    key_vectors,
    value_vectors,
    log_decay,
    write_strength,
    output_gate,
    norm_gain,
    out_proj,
):
    rows, wide = query_vectors.shape
    depth, width = out_proj.shape
    vmem = pl.BlockSpec(memory_space=pltpu.VMEM)
    anywhere = pl.BlockSpec(memory_space=pl.ANY)
    dma = pltpu.SemaphoreType.DMA
    half = DEEP // 2
    return pl.pallas_call(
        kernel,
        out_shape=jax.ShapeDtypeStruct((rows // FANS, width), BF16),
        in_specs=[vmem] * 6 + [anywhere] * 2,
        out_specs=vmem,
        scratch_shapes=[
            pltpu.VMEM((rows, wide), BF16),
            pltpu.VMEM((depth, width), BF16),
            pltpu.VMEM((HEADS, MSG, N), BF16),
            pltpu.VMEM((ROW, MSG, N), BF16),
            pltpu.VMEM((ROW * N, N), BF16),
            pltpu.VMEM((ROW, N, N), F32),
            pltpu.VMEM((ROW, 8, N), F32),
            pltpu.VMEM((DEEP, MSG, N), BF16),
            pltpu.VMEM((ROW, N, N), BF16),
            pltpu.VMEM((HEADS, N, N), BF16),
            pltpu.VMEM((HEADS, N, N), F32),
            pltpu.VMEM((HEADS, N, N), F32),
            pltpu.VMEM((rows, wide), BF16),
            pltpu.VMEM((CHUNKS, rows, width // CHUNKS), BF16),
            pltpu.VMEM((CHUNKS, FANS, rows // FANS, width // CHUNKS), BF16),
            dma((2,)),
            dma((HEADS,)),
            dma((ROW,)),
            dma((half,)),
            dma((half,)),
            dma((half - 1,)),
            dma((half - 1,)),
            dma((ROW,)),
            dma((HEADS,)),
            dma((CHUNKS, FANS - 1)),
            dma((CHUNKS, FANS)),
        ],
        compiler_params=pltpu.CompilerParams(
            collective_id=0, has_side_effects=True, vmem_limit_bytes=50 * 1024 * 1024
        ),
        cost_estimate=pl.CostEstimate(
            flops=2_000_000_000, bytes_accessed=6_000_000, transcendentals=500_000
        ),
    )(
        query_vectors,
        key_vectors,
        value_vectors,
        log_decay,
        write_strength,
        norm_gain.reshape(1, N),
        output_gate,
        out_proj,
    )


def solution(mesh):
    in_specs = (
        P("seq", "head"),
        P("seq", "head"),
        P("seq", "head"),
        P("head", "seq"),
        P("head", "seq"),
        P("seq", "head"),
        P(),
        P("head", None),
    )
    out_specs = P(("seq", "head"), None)
    return jax.shard_map(
        on_device, mesh=mesh, in_specs=in_specs, out_specs=out_specs, check_vma=False
    )
```

time: 553 us -> 58.8 us (0.11)
  the two profiles are of different devices: /device:TPU:224 before, /device:TPU:1 now
where the time goes in v1:
time: 58.8 us; the launch traced here: 58.5 us
  Pallas kernels  52 us (88%)
  local copies, waits for them, and re-layouts  6.49 us (11%)
    pallas_call x1, Pallas kernels, on_device(): pl.pallas_call(kernel, out_shape=jax.ShapeDtypeStruct((rows // FANS, widt...  52 us
    unnamed x15, local copies, waits for them, and re-layouts  6.49 us

profile of v1, /device:TPU:1, one launch (start us, length us, event | category | flops | bytes accessed | tf_op | source)
XLA Modules:
  0.0 58.5 jit_solution(17276020954202768765)
XLA Ops:
  0.0 0.0 copy-start
  0.0 0.9 %copy-done = bf16[128,1024]{1,0:T(8,128)(2,1)S(1)} copy-done((bf16[128,1024]{1,0:T(8,128)(2,1)S(1)}, bf16[128,1024]{1,0:T(8,128)(2,1)}, u32[]{:S(2)}) %copy-start) | copy-done | bytes 262168
  1.0 0.0 copy-start.1
  1.0 0.9 %copy-done.1 = bf16[128,1024]{1,0:T(8,128)(2,1)S(1)} copy-done((bf16[128,1024]{1,0:T(8,128)(2,1)S(1)}, bf16[128,1024]{1,0:T(8,128)(2,1)}, u32[]{:S(2)}) %copy-start.1) | copy-done | bytes 262168
  1.9 0.0 copy-start.2
  1.9 0.9 %copy-done.2 = bf16[128,1024]{1,0:T(8,128)(2,1)S(1)} copy-done((bf16[128,1024]{1,0:T(8,128)(2,1)S(1)}, bf16[128,1024]{1,0:T(8,128)(2,1)}, u32[]{:S(2)}) %copy-start.2) | copy-done | bytes 262168
  2.9 0.0 copy-start.3
  2.9 0.9 %copy-done.3 = bf16[128,1024]{1,0:T(8,128)(2,1)S(1)} copy-done((bf16[128,1024]{1,0:T(8,128)(2,1)S(1)}, bf16[128,1024]{1,0:T(8,128)(2,1)}, u32[]{:S(2)}) %copy-start.3) | copy-done | bytes 262168
  3.8 0.0 copy-start.4
  3.8 0.7 %copy-done.4 = f32[8,128]{1,0:T(8,128)S(1)} copy-done((f32[8,128]{1,0:T(8,128)S(1)}, f32[8,128]{1,0:T(8,128)}, u32[]{:S(2)}) %copy-start.4) | copy-done | bytes 4120
  4.5 0.0 copy-start.5
  4.5 0.7 %copy-done.5 = f32[8,128]{1,0:T(8,128)S(1)} copy-done((f32[8,128]{1,0:T(8,128)S(1)}, f32[8,128]{1,0:T(8,128)}, u32[]{:S(2)}) %copy-start.5) | copy-done | bytes 4120
  5.2 0.0 copy-start.6
  5.2 0.7 %copy-done.6 = f32[128]{0:T(128)S(1)} copy-done((f32[128]{0:T(128)S(1)}, f32[128]{0:T(128)}, u32[]{:S(2)}) %copy-start.6) | copy-done | bytes 536
  5.8 52.0 %shard_map.82 = bf16[32,2304]{1,0:T(8,128)(2,1)S(1)} custom-call(bf16[128,1024]{1,0:T(8,128)(2,1)S(1)} %copy-done, bf16[128,1024]{1,0:T(8,128)(2,1)S(1)} %copy-done.1, bf16[128,1024]{1,0:T(8,128)(2,1)S(1)} %copy-done.2, f32[8,128]{1,0:T(8,128)S(1)} %copy-done.4, f32[8,128]{1,0:T(8,128)S(1)} %copy-done.5, f32[1,128]{1,0:T(1,128)S(1)} %bitcast.1, ...), custom_call_target="tpu_custom_call" | custom-call | flops 2000000000 | bytes 6000000 | tf_op jit(solution)/shard_map/pallas_call | solution.py:412
  57.9 0.7 %copy.10 = bf16[32,2304]{1,0:T(8,128)(2,1)} copy(bf16[32,2304]{1,0:T(8,128)(2,1)S(1)} %shard_map.82) | data formatting | bytes 294912
Async XLA Ops:
  0.0 0.9 %copy-start = (bf16[128,1024]{1,0:T(8,128)(2,1)S(1)}, bf16[128,1024]{1,0:T(8,128)(2,1)}, u32[]{:S(2)}) copy-start(bf16[128,1024]{1,0:T(8,128)(2,1)} %q_ref.1) | copy-start | bytes 786436
  1.0 0.9 %copy-start.1 = (bf16[128,1024]{1,0:T(8,128)(2,1)S(1)}, bf16[128,1024]{1,0:T(8,128)(2,1)}, u32[]{:S(2)}) copy-start(bf16[128,1024]{1,0:T(8,128)(2,1)} %k_ref.1) | copy-start | bytes 786436
  1.9 0.9 %copy-start.2 = (bf16[128,1024]{1,0:T(8,128)(2,1)S(1)}, bf16[128,1024]{1,0:T(8,128)(2,1)}, u32[]{:S(2)}) copy-start(bf16[128,1024]{1,0:T(8,128)(2,1)} %v_ref.1) | copy-start | bytes 786436
  2.9 0.9 %copy-start.3 = (bf16[128,1024]{1,0:T(8,128)(2,1)S(1)}, bf16[128,1024]{1,0:T(8,128)(2,1)}, u32[]{:S(2)}) copy-start(bf16[128,1024]{1,0:T(8,128)(2,1)} %gate_any.1) | copy-start | bytes 786436
  3.8 0.7 %copy-start.4 = (f32[8,128]{1,0:T(8,128)S(1)}, f32[8,128]{1,0:T(8,128)}, u32[]{:S(2)}) copy-start(f32[8,128]{1,0:T(8,128)} %decay_ref.1) | copy-start | bytes 12292
  4.5 0.7 %copy-start.5 = (f32[8,128]{1,0:T(8,128)S(1)}, f32[8,128]{1,0:T(8,128)}, u32[]{:S(2)}) copy-start(f32[8,128]{1,0:T(8,128)} %strength_ref.1) | copy-start | bytes 12292
  5.2 0.7 %copy-start.6 = (f32[128]{0:T(128)S(1)}, f32[128]{0:T(128)}, u32[]{:S(2)}) copy-start(f32[128]{0:T(128)} %param.14) | copy-start | bytes 1540

commit v2 on v1

v2 whole, which is shorter than its diff:
```python
import jax
import jax.numpy as jnp
from jax import lax
from jax.experimental import pallas as pl
from jax.experimental.pallas import tpu as pltpu
from jax.sharding import PartitionSpec as P

MESH = pl.DeviceIdType.MESH
F32 = jnp.float32
BF16 = jnp.bfloat16

ROW = 8
GROUP = 16
GROUPS = 4
FANS = 4
HEADS = 8
BATCH = 4
N = 128
GROWS = 16
MSG = GROWS + 2 * N
CHUNKS = 3
OWNERS = tuple(ROW * ((h % 4 + h // 4 + 1) % 2) + 2 * (h % 4) for h in range(HEADS))
EPS = 1e-06


def bdot(left, right, dims):
    return lax.dot_general(
        left.astype(BF16), right.astype(BF16), (dims, ((0,), (0,))), preferred_element_type=F32
    )


NN = ((2,), (1,))
NT = ((2,), (2,))
TN = ((1,), (1,))


def split(x):
    high = x.astype(BF16)
    return high, (x - high.astype(F32)).astype(BF16)


def bdot_left(left, right, dims=NN):
    high, low = split(left)
    return bdot(high, right, dims) + bdot(low, right, dims)


def bdot_right(left, right, dims=NN):
    high, low = split(right)
    return bdot(left, high, dims) + bdot(left, low, dims)


def bdot_both(left, right, dims=NN):
    lh, ll = split(left)
    rh, rl = split(right)
    return bdot(lh, rh, dims) + (bdot(lh, rl, dims) + bdot(ll, rh, dims))


def dot(left, right):
    return jnp.dot(left.astype(BF16), right.astype(BF16), preferred_element_type=F32)


def dot_left(left, right):
    high, low = split(left)
    return dot(high, right) + dot(low, right)


def dot_right(left, right):
    high, low = split(right)
    return dot(left, high) + dot(left, low)


def dot_both(left, right):
    lh, ll = split(left)
    rh, rl = split(right)
    return dot(lh, rh) + (dot(lh, rl) + dot(ll, rh))


def inverse(couple, row, col):
    def level(size):
        pair = (row // (2 * size)) == (col // (2 * size))
        return pair & ((row // size) % 2 == 1) & ((col // size) % 2 == 0)

    eye = jnp.where(row == col, 1.0, 0.0).astype(F32)
    solved = eye - jnp.where(level(1), couple, 0.0)
    size = 2
    while size < N:
        below = jnp.where(level(size), couple, 0.0)
        solved = solved - bdot(solved, bdot(below, solved, NN), NN)
        size *= 2
    rest = (eye - solved) - bdot_both(couple, solved)
    return solved + bdot(solved, rest, NN)


def local_terms(keyrow, value, cum_row, cum_col, str_row, str_col):
    shape = keyrow.shape
    row = lax.broadcasted_iota(jnp.int32, shape, 1)
    col = lax.broadcasted_iota(jnp.int32, shape, 2)
    keykey = bdot(keyrow, keyrow, NT)
    diag = jnp.where(row == col, keykey, 0.0)
    kscale_row = lax.rsqrt(jnp.sum(diag, axis=1, keepdims=True) + EPS)
    kscale_col = lax.rsqrt(jnp.sum(diag, axis=2, keepdims=True) + EPS)
    ratio = jnp.where(row >= col, jnp.exp(jnp.minimum(cum_col - cum_row, 0.0)), 0.0) * kscale_row
    couple = jnp.where(row > col, ratio * keykey, 0.0) * (str_col * kscale_col)
    solved = inverse(couple, row, col)
    from_value = bdot_left(solved * str_row, value)
    from_key = bdot_left(solved * (str_row * jnp.exp(cum_row) * kscale_row), keyrow)
    both = jnp.concatenate([from_key, from_value], axis=2)
    last = cum_row[:, :, N - 1 :]
    tail = jnp.exp(last - cum_col) * kscale_col
    ends = bdot_right(keyrow, both * tail, TN)
    return ratio, both, ends, jnp.exp(last)


def local_reads(query, keyrow, ratio, both, cum_col):
    query32 = query.astype(F32)
    qscale = lax.rsqrt(jnp.sum(query32 * query32, axis=2, keepdims=True) + EPS)
    score = ratio * bdot(query, keyrow, NT) * qscale
    read = bdot_both(score, both)
    reach = query32 * (jnp.exp(cum_col) * qscale) - read[:, :, :N]
    return reach, read[:, :, N:]


def decay_rows(gain):
    place = lax.broadcasted_iota(jnp.int32, (GROWS, N), 0)
    high = gain.astype(BF16).astype(F32)
    middle = (gain - high).astype(BF16).astype(F32)
    low = gain - high - middle
    rows = jnp.where(place == 0, high, jnp.where(place == 1, middle, jnp.where(place == 2, low, 0.0)))
    return rows.astype(BF16)


def read_message(buffer, index):
    gain = jnp.sum(buffer[index, N : N + GROWS, :].astype(F32), axis=0, keepdims=True)
    return gain, buffer[index, N + GROWS :, :], buffer[index, :N, :]


def advance(run, step):
    run_g, run_d, run_j = run
    step_g, step_d, step_j = step
    prod = dot_right(step_d, jnp.concatenate([run_d, run_j], axis=1))
    return (
        run_g * step_g,
        step_g * run_d + run_g * step_d.astype(F32) + prod[:, :N],
        step_g * run_j + step_j.astype(F32) + prod[:, N:],
    )


def kernel(
    q_any,
    k_any,
    v_any,
    decay_any,
    strength_any,
    gate_any,
    gain_any,
    proj_any,
    out_ref,
    q_buf,
    k_buf,
    v_buf,
    decay_buf,
    strength_buf,
    gate_buf,
    gain_buf,
    proj_buf,
    head_send,
    head_recv,
    pre_d,
    pre_j,
    pre_g,
    total_buf,
    state_buf,
    state_send,
    state_recv,
    reach_buf,
    local_buf,
    normed_buf,
    part_buf,
    part_recv,
    load_sem,
    hs_sem,
    hr_sem,
    ts_sem,
    tr_sem,
    ss_sem,
    sr_sem,
    ps_sem,
    pr_sem,
):
    place = lax.axis_index("seq")
    fan = lax.axis_index("head")
    group = place // GROUP
    mine = lax.rem(place, GROUP)
    base = group * GROUP
    chip = lax.rem(mine, ROW) // 2
    owner = lax.rem(mine, 2) == 0
    own_head = chip + 4 * (1 - lax.rem(mine // ROW + chip, 2))
    peers = [lax.rem(mine + step, GROUP) for step in range(1, GROUP)]
    fan_peers = [lax.rem(fan + step, FANS) for step in (2, 1, 3)]

    loads = [
        pltpu.make_async_copy(source, target, load_sem.at[n])
        for n, (source, target) in enumerate(
            (
                (k_any, k_buf),
                (decay_any, decay_buf),
                (strength_any, strength_buf),
                (v_any, v_buf),
                (q_any, q_buf),
                (gate_any, gate_buf),
                (gain_any, gain_buf),
                (proj_any, proj_buf),
            )
        )
    ]
    for load in loads:
        load.start()

    barrier = pltpu.get_barrier_semaphore()
    greeted = [(base + peer, fan) for peer in peers]
    greeted += [(lax.rem(place + step * GROUP, GROUPS * GROUP), fan) for step in range(1, GROUPS)]
    greeted += [(place, peer) for peer in fan_peers]
    for device in greeted:
        pl.semaphore_signal(barrier, inc=1, device_id=device, device_id_type=MESH)

    def remote(source, target, send, recv, device):
        return pltpu.make_async_remote_copy(
            src_ref=source,
            dst_ref=target,
            send_sem=send,
            recv_sem=recv,
            device_id=device,
            device_id_type=MESH,
        )

    def head_copy(h, sender):
        return remote(
            head_send.at[h],
            head_recv.at[sender],
            hs_sem.at[h],
            hr_sem.at[sender],
            (base + OWNERS[h], fan),
        )

    def total_copy(source, target):
        rows = N if source == 0 else MSG
        return remote(
            total_buf.at[source, pl.ds(0, rows)],
            total_buf.at[source, pl.ds(0, rows)],
            ts_sem.at[target],
            tr_sem.at[source],
            (target * GROUP + mine, fan),
        )

    def state_copy(peer):
        return remote(
            state_send.at[peer],
            state_recv.at[own_head],
            ss_sem.at[peer],
            sr_sem.at[own_head],
            (base + peer, fan),
        )

    tri_row = lax.broadcasted_iota(jnp.int32, (N, N), 0)
    tri_col = lax.broadcasted_iota(jnp.int32, (N, N), 1)
    upper = jnp.where(tri_row <= tri_col, 1.0, 0.0).astype(F32)
    for load in loads[1:3]:
        load.wait()
    strength = strength_buf[...]
    cumul = jnp.dot(
        decay_buf[...], upper, precision=lax.Precision.HIGHEST, preferred_element_type=F32
    )
    turned = jnp.concatenate([cumul, strength, jnp.zeros((N - 2 * HEADS, N), F32)], axis=0).T
    loads[0].wait()
    loads[3].wait()
    kept = []
    for start in range(0, HEADS, BATCH):
        heads = range(start, start + BATCH)

        def per_head(buf):
            return jnp.stack([buf[:, h * N : (h + 1) * N] for h in heads])

        cum_row = jnp.stack([cumul[h : h + 1, :] for h in heads])
        str_row = jnp.stack([strength[h : h + 1, :] for h in heads])
        cum_col = jnp.stack([turned[:, h : h + 1] for h in heads])
        str_col = jnp.stack([turned[:, HEADS + h : HEADS + h + 1] for h in heads])
        keyrow = per_head(k_buf)
        ratio, both, ends, last = local_terms(
            keyrow, per_head(v_buf), cum_row, cum_col, str_row, str_col
        )
        kept.append((heads, keyrow, ratio, both, cum_col))
        head_send[start : start + BATCH, N + GROWS :, :] = (-ends[:, :, :N]).astype(BF16)
        head_send[start : start + BATCH, :N, :] = ends[:, :, N:].astype(BF16)
        for n, h in enumerate(heads):
            head_send[h, N : N + GROWS, :] = decay_rows(jnp.broadcast_to(last[n], (GROWS, N)))

        if start == 0:
            pl.semaphore_wait(barrier, len(greeted))
        for h in heads:

            @pl.when(mine != OWNERS[h])
            def _():
                head_copy(h, mine).start()

    loads[4].wait()
    for heads, keyrow, ratio, both, cum_col in kept:
        query = jnp.stack([q_buf[:, h * N : (h + 1) * N] for h in heads])
        reach, local = local_reads(query, keyrow, ratio, both, cum_col)
        reach_buf[heads.start : heads.stop] = reach
        local_buf[heads.start : heads.stop] = local

    @pl.when(owner)
    def _():
        head_recv[mine] = head_send[own_head]
        runs = [None, None]
        for i in range(ROW):
            for n in range(2):
                at = n * ROW + i

                @pl.when(mine != at)
                def _():
                    head_copy(0, at).wait_recv()

                step = read_message(head_recv, at)
                if i == 0:
                    pre_g[at] = jnp.ones((8, N), F32)
                    pre_d[pl.ds(at * N, N), :] = jnp.zeros((N, N), BF16)
                    pre_j[at] = jnp.zeros((N, N), F32)
                    runs[n] = (step[0], step[1].astype(F32), step[2].astype(F32))
                else:
                    run_g, run_d, run_j = runs[n]
                    pre_g[at] = jnp.broadcast_to(run_g, (8, N))
                    pre_d[pl.ds(at * N, N), :] = run_d.astype(BF16)
                    pre_j[at] = run_j
                    runs[n] = advance(runs[n], step)
        (first_g, first_d, first_j), (second_g, second_d, second_j) = runs
        prod = dot_both(second_d, jnp.concatenate([first_d, first_j], axis=1))
        total_buf[group, :N, :] = (second_g * first_j + second_j + prod[:, N:]).astype(BF16)
        total_buf[group, N : N + GROWS, :] = decay_rows(
            jnp.broadcast_to(first_g * second_g, (GROWS, N))
        )
        total_buf[group, N + GROWS :, :] = (
            second_g * first_d + first_g * second_d + prod[:, :N]
        ).astype(BF16)

        for source in range(GROUPS - 1):

            @pl.when(group == source)
            def _():
                for target in range(source + 1, GROUPS):
                    total_copy(source, target).start()

        state_buf[...] = jnp.zeros((N, N), F32)
        for source in range(GROUPS - 1):

            @pl.when(group > source)
            def _():
                total_copy(source, source + 1).wait_recv()
                if source == 0:
                    state_buf[...] = total_buf[0, :N, :].astype(F32)
                else:
                    gain, step_d, step_j = read_message(total_buf, source)
                    state = state_buf[...]
                    state_buf[...] = (
                        gain * state + dot_right(step_d, state) + step_j.astype(F32)
                    )

        state = state_buf[...]
        for n in range(2):
            starts = dot(pre_d[n * ROW * N : (n + 1) * ROW * N, :], state)
            for i in range(ROW):
                at = n * ROW + i
                moved = pre_g[at, :1, :] * state + starts[i * N : (i + 1) * N] + pre_j[at]
                state_send[at] = moved.astype(BF16)
            state = first_g * state + dot_left(first_d, state) + first_j
        for peer in peers:
            state_copy(peer).start()
        state_recv[own_head] = state_send[mine]

    loads[5].wait()
    loads[6].wait()
    gating = jax.nn.sigmoid(gate_buf[...].astype(F32)) * jnp.tile(gain_buf[...], (1, HEADS))
    for h in range(HEADS):

        @pl.when(mine != OWNERS[h])
        def _():
            remote(
                state_send.at[h],
                state_recv.at[h],
                ss_sem.at[h],
                sr_sem.at[h],
                (base + OWNERS[h], fan),
            ).wait_recv()

    outputs = bdot_left(reach_buf[...], state_recv[...]) + local_buf[...]
    square = jnp.mean(outputs * outputs, axis=2, keepdims=True)
    outputs = outputs * lax.rsqrt(square + EPS)
    for h in range(HEADS):
        columns = slice(h * N, (h + 1) * N)
        normed_buf[:, columns] = (outputs[h] * gating[:, columns]).astype(BF16)

    loads[7].wait()
    rows = N // FANS
    width = proj_buf.shape[1] // CHUNKS

    def part_copy(c, n, owner_fan, peer):
        return remote(
            part_buf.at[c, pl.ds(pl.multiple_of(peer * rows, rows), rows), :],
            part_recv.at[c, owner_fan],
            ps_sem.at[c, n],
            pr_sem.at[c, owner_fan],
            (place, peer),
        )

    for c in range(CHUNKS):
        part_buf[c] = jnp.dot(
            normed_buf[...],
            proj_buf[:, c * width : (c + 1) * width],
            preferred_element_type=F32,
        ).astype(BF16)
        for n, peer in enumerate(fan_peers):
            part_copy(c, n, fan, peer).start()
        part_recv[c, fan] = part_buf[c, pl.ds(pl.multiple_of(fan * rows, rows), rows), :]
    for c in range(CHUNKS):
        for n, peer in enumerate(fan_peers):
            part_copy(c, n, peer, peer).wait_recv()
        summed = part_recv[c, 0].astype(F32)
        for n in range(1, FANS):
            summed = summed + part_recv[c, n].astype(F32)
        out_ref[:, c * width : (c + 1) * width] = summed.astype(BF16)

    for h in range(HEADS):

        @pl.when(mine != OWNERS[h])
        def _():
            head_copy(h, mine).wait_send()

    @pl.when(owner)
    def _():
        for source in range(GROUPS - 1):

            @pl.when(group == source)
            def _():
                for target in range(source + 1, GROUPS):
                    total_copy(source, target).wait_send()

        for peer in peers:
            state_copy(peer).wait_send()

    for c in range(CHUNKS):
        for n, peer in enumerate(fan_peers):
            part_copy(c, n, fan, peer).wait_send()


def on_device(
    query_vectors,
    key_vectors,
    value_vectors,
    log_decay,
    write_strength,
    output_gate,
    norm_gain,
    out_proj,
):
    rows, wide = query_vectors.shape
    depth, width = out_proj.shape
    dma = pltpu.SemaphoreType.DMA
    return pl.pallas_call(
        kernel,
        out_shape=jax.ShapeDtypeStruct((rows // FANS, width), BF16),
        in_specs=[pl.BlockSpec(memory_space=pltpu.HBM)] * 8,
        out_specs=pl.BlockSpec(memory_space=pltpu.VMEM),
        scratch_shapes=[
            pltpu.VMEM((rows, wide), BF16),
            pltpu.VMEM((rows, wide), BF16),
            pltpu.VMEM((rows, wide), BF16),
            pltpu.VMEM((HEADS, N), F32),
            pltpu.VMEM((HEADS, N), F32),
            pltpu.VMEM((rows, wide), BF16),
            pltpu.VMEM((1, N), F32),
            pltpu.VMEM((depth, width), BF16),
            pltpu.VMEM((HEADS, MSG, N), BF16),
            pltpu.VMEM((GROUP, MSG, N), BF16),
            pltpu.VMEM((GROUP * N, N), BF16),
            pltpu.VMEM((GROUP, N, N), F32),
            pltpu.VMEM((GROUP, 8, N), F32),
            pltpu.VMEM((GROUPS, MSG, N), BF16),
            pltpu.VMEM((N, N), F32),
            pltpu.VMEM((GROUP, N, N), BF16),
            pltpu.VMEM((HEADS, N, N), BF16),
            pltpu.VMEM((HEADS, N, N), F32),
            pltpu.VMEM((HEADS, N, N), F32),
            pltpu.VMEM((rows, wide), BF16),
            pltpu.VMEM((CHUNKS, rows, width // CHUNKS), BF16),
            pltpu.VMEM((CHUNKS, FANS, rows // FANS, width // CHUNKS), BF16),
            dma((8,)),
            dma((HEADS,)),
            dma((GROUP,)),
            dma((GROUPS,)),
            dma((GROUPS,)),
            dma((GROUP,)),
            dma((HEADS,)),
            dma((CHUNKS, FANS - 1)),
            dma((CHUNKS, FANS)),
        ],
        compiler_params=pltpu.CompilerParams(
            collective_id=0, has_side_effects=True, vmem_limit_bytes=64 * 1024 * 1024
        ),
        cost_estimate=pl.CostEstimate(
            flops=2_000_000_000, bytes_accessed=6_000_000, transcendentals=500_000
        ),
    )(
        query_vectors,
        key_vectors,
        value_vectors,
        log_decay,
        write_strength,
        output_gate,
        norm_gain.reshape(1, N),
        out_proj,
    )


def solution(mesh):
    in_specs = (
        P("seq", "head"),
        P("seq", "head"),
        P("seq", "head"),
        P("head", "seq"),
        P("head", "seq"),
        P("seq", "head"),
        P(),
        P("head", None),
    )
    out_specs = P(("seq", "head"), None)
    return jax.shard_map(
        on_device, mesh=mesh, in_specs=in_specs, out_specs=out_specs, check_vma=False
    )
```

time: 58.8 us -> 43.1 us (0.73)
  the two profiles are of different devices: /device:TPU:1 before, /device:TPU:224 now
where the time goes in v2:
time: 43.1 us; the launch traced here: 42.6 us
  Pallas kernels  41 us (95%)
  local copies, waits for them, and re-layouts  1.58 us (4%)
    pallas_call x1, Pallas kernels, on_device(): pl.pallas_call(kernel, out_shape=jax.ShapeDtypeStruct((rows // FANS, widt...  41 us
    unnamed x1, local copies, waits for them, and re-layouts  1.58 us

profile of v2, /device:TPU:224, one launch (start us, length us, event | category | flops | bytes accessed | tf_op | source)
XLA Modules:
  0.0 42.6 jit_solution(13054326636998405601)
XLA Ops:
  0.0 41.0 %shard_map.82 = bf16[32,2304]{1,0:T(8,128)(2,1)} custom-call(bf16[128,1024]{1,0:T(8,128)(2,1)} %q_any.1, bf16[128,1024]{1,0:T(8,128)(2,1)} %k_any.1, bf16[128,1024]{1,0:T(8,128)(2,1)} %v_any.1, f32[8,128]{1,0:T(8,128)} %decay_any.1, f32[8,128]{1,0:T(8,128)} %strength_any.1, bf16[128,1024]{1,0:T(8,128)(2,1)} %gate_any.1, f32[1,128]{1,0:T(1,128)} %bitcast.1, ...), custom_call_target="tpu_custom_call" | custom-call | flops 2000000000 | bytes 6000000 | tf_op jit(solution)/shard_map/pallas_call | solution.py:468
  41.1 1.6 %copy.10 = bf16[32,2304]{1,0:T(8,128)(2,1)} copy(bf16[32,2304]{1,0:T(8,128)(2,1)} %shard_map.82) | data formatting | bytes 294912

commit v3 on v2

--- a/solution.py
+++ b/solution.py
@@ -12,9 +12,11 @@
 ROW = 8
 GROUP = 16
 GROUPS = 4
+QUARTERS = 4
+QUARTER = GROUP // QUARTERS
 FANS = 4
 HEADS = 8
-BATCH = 4
+BATCH = 8
 N = 128
 GROWS = 16
 MSG = GROWS + 2 * N
@@ -22,6 +24,8 @@
 OWNERS = tuple(ROW * ((h % 4 + h // 4 + 1) % 2) + 2 * (h % 4) for h in range(HEADS))
 EPS = 1e-06
 
+FARTHEST = (4, 12, 5, 13, 3, 11, 2, 10, 6, 14, 7, 15, 1, 9, 8)
+
 
 def bdot(left, right, dims):
     return lax.dot_general(
@@ -39,76 +43,106 @@
     return high, (x - high.astype(F32)).astype(BF16)
 
 
-def bdot_left(left, right, dims=NN):
-    high, low = split(left)
-    return bdot(high, right, dims) + bdot(low, right, dims)
-
-
-def bdot_right(left, right, dims=NN):
-    high, low = split(right)
-    return bdot(left, high, dims) + bdot(left, low, dims)
-
-
-def bdot_both(left, right, dims=NN):
+def bdot_left(left, right):
+    return bdot(jnp.concatenate(split(left), axis=2), jnp.concatenate([right, right], axis=1), NN)
+
+
+def bdot_right_turned(left, right):
+    return bdot(
+        jnp.concatenate([left, left], axis=1), jnp.concatenate(split(right), axis=1), TN
+    )
+
+
+def bdot_both(left, right):
     lh, ll = split(left)
     rh, rl = split(right)
-    return bdot(lh, rh, dims) + (bdot(lh, rl, dims) + bdot(ll, rh, dims))
+    return bdot(
+        jnp.concatenate([lh, ll, lh], axis=2), jnp.concatenate([rh, rh, rl], axis=1), NN
+    )
 
 
 def dot(left, right):
     return jnp.dot(left.astype(BF16), right.astype(BF16), preferred_element_type=F32)
 
 
-def dot_left(left, right):
-    high, low = split(left)
-    return dot(high, right) + dot(low, right)
+def dot_turned(left, right):
+    return lax.dot_general(
+        left.astype(BF16), right.astype(BF16), (((1,), (1,)), ((), ())), preferred_element_type=F32
+    )
+
+
+def thirds(x):
+    high = x.astype(BF16)
+    rest = x - high.astype(F32)
+    middle = rest.astype(BF16)
+    return high, middle, (rest - middle.astype(F32)).astype(BF16)
 
 
 def dot_right(left, right):
-    high, low = split(right)
-    return dot(left, high) + dot(left, low)
+    return dot(jnp.concatenate([left, left], axis=1), jnp.concatenate(split(right), axis=0))
 
 
 def dot_both(left, right):
     lh, ll = split(left)
     rh, rl = split(right)
-    return dot(lh, rh) + (dot(lh, rl) + dot(ll, rh))
-
-
-def inverse(couple, row, col):
-    def level(size):
-        pair = (row // (2 * size)) == (col // (2 * size))
-        return pair & ((row // size) % 2 == 1) & ((col // size) % 2 == 0)
-
-    eye = jnp.where(row == col, 1.0, 0.0).astype(F32)
-    solved = eye - jnp.where(level(1), couple, 0.0)
+    return dot(jnp.concatenate([lh, ll, lh], axis=1), jnp.concatenate([rh, rh, rl], axis=0))
+
+
+def places():
+    shape = (1, N, N)
+    return lax.broadcasted_iota(jnp.int32, shape, 1), lax.broadcasted_iota(jnp.int32, shape, 2)
+
+
+def mask(where):
+    return jnp.where(where, 1.0, 0.0).astype(F32)
+
+
+def inverse(couple):
+    row, col = places()
+
+    def between(size, count):
+        return mask(
+            ((row // (count * size)) == (col // (count * size))) & ((row // size) > (col // size))
+        )
+
+    eye = mask(row == col)
+    solved = eye - couple * between(1, 2)
     size = 2
     while size < N:
-        below = jnp.where(level(size), couple, 0.0)
-        solved = solved - bdot(solved, bdot(below, solved, NN), NN)
-        size *= 2
-    rest = (eye - solved) - bdot_both(couple, solved)
-    return solved + bdot(solved, rest, NN)
-
-
-def local_terms(keyrow, value, cum_row, cum_col, str_row, str_col):
-    shape = keyrow.shape
-    row = lax.broadcasted_iota(jnp.int32, shape, 1)
-    col = lax.broadcasted_iota(jnp.int32, shape, 2)
+        near = solved.astype(BF16)
+        step = bdot(near, couple * between(size, 4), NN).astype(BF16)
+        prod = bdot(step, jnp.concatenate([step, near], axis=2), NN)
+        solved = solved - prod[:, :, N:]
+        solved = solved + bdot(prod[:, :, :N], solved, NN)
+        size *= 4
+    near = solved.astype(BF16)
+    solved = near.astype(F32)
+    rest = (eye - solved) - bdot_left(couple, near)
+    return solved + bdot(near, rest, NN)
+
+
+def local_solve(keyrow, cum_row, cum_col, str_row, str_col):
+    row, col = places()
     keykey = bdot(keyrow, keyrow, NT)
-    diag = jnp.where(row == col, keykey, 0.0)
+    diag = keykey * mask(row == col)
     kscale_row = lax.rsqrt(jnp.sum(diag, axis=1, keepdims=True) + EPS)
     kscale_col = lax.rsqrt(jnp.sum(diag, axis=2, keepdims=True) + EPS)
-    ratio = jnp.where(row >= col, jnp.exp(jnp.minimum(cum_col - cum_row, 0.0)), 0.0) * kscale_row
-    couple = jnp.where(row > col, ratio * keykey, 0.0) * (str_col * kscale_col)
-    solved = inverse(couple, row, col)
-    from_value = bdot_left(solved * str_row, value)
-    from_key = bdot_left(solved * (str_row * jnp.exp(cum_row) * kscale_row), keyrow)
-    both = jnp.concatenate([from_key, from_value], axis=2)
+    ratio = jnp.exp(jnp.minimum(cum_col - cum_row, 0.0)) * mask(row >= col) * kscale_row
+    couple = ratio * keykey * mask(row > col) * (str_col * kscale_col)
+    solved = inverse(couple)
     last = cum_row[:, :, N - 1 :]
-    tail = jnp.exp(last - cum_col) * kscale_col
-    ends = bdot_right(keyrow, both * tail, TN)
-    return ratio, both, ends, jnp.exp(last)
+    return (
+        solved * (str_row * jnp.exp(cum_row) * kscale_row),
+        solved * str_row,
+        ratio,
+        jnp.exp(last - cum_col) * kscale_col,
+        jnp.exp(last),
+    )
+
+
+def local_ends(keyrow, value, for_key, for_value, tail):
+    both = jnp.concatenate([bdot_left(for_key, keyrow), bdot_left(for_value, value)], axis=2)
+    return both, bdot_right_turned(keyrow, both * tail)
 
 
 def local_reads(query, keyrow, ratio, both, cum_col):
@@ -142,6 +176,17 @@
         run_g * step_g,
         step_g * run_d + run_g * step_d.astype(F32) + prod[:, :N],
         step_g * run_j + step_j.astype(F32) + prod[:, N:],
+    )
+
+
+def join(run, step):
+    run_g, run_d, run_j = run
+    step_g, step_d, step_j = step
+    prod = dot_both(step_d, jnp.concatenate([run_d, run_j], axis=1))
+    return (
+        run_g * step_g,
+        step_g * run_d + run_g * step_d + prod[:, :N],
+        step_g * run_j + step_j + prod[:, N:],
     )
 
 
@@ -261,36 +306,33 @@
             (base + peer, fan),
         )
 
-    tri_row = lax.broadcasted_iota(jnp.int32, (N, N), 0)
-    tri_col = lax.broadcasted_iota(jnp.int32, (N, N), 1)
-    upper = jnp.where(tri_row <= tri_col, 1.0, 0.0).astype(F32)
-    for load in loads[1:3]:
+    for load in loads[:4]:
         load.wait()
+    row, col = places()
+    below = mask(row[0] >= col[0])
+    decays, strengths = thirds(decay_buf[...]), thirds(strength_buf[...])
+    cumul = sum(dot_turned(third, below) for third in decays)
+    cumul_turned = sum(dot_turned(below, third) for third in decays)
     strength = strength_buf[...]
-    cumul = jnp.dot(
-        decay_buf[...], upper, precision=lax.Precision.HIGHEST, preferred_element_type=F32
-    )
-    turned = jnp.concatenate([cumul, strength, jnp.zeros((N - 2 * HEADS, N), F32)], axis=0).T
-    loads[0].wait()
-    loads[3].wait()
+    strength_turned = sum(dot_turned(mask(row[0] == col[0]), third) for third in strengths)
     kept = []
     for start in range(0, HEADS, BATCH):
         heads = range(start, start + BATCH)
-
-        def per_head(buf):
-            return jnp.stack([buf[:, h * N : (h + 1) * N] for h in heads])
-
         cum_row = jnp.stack([cumul[h : h + 1, :] for h in heads])
         str_row = jnp.stack([strength[h : h + 1, :] for h in heads])
-        cum_col = jnp.stack([turned[:, h : h + 1] for h in heads])
-        str_col = jnp.stack([turned[:, HEADS + h : HEADS + h + 1] for h in heads])
-        keyrow = per_head(k_buf)
-        ratio, both, ends, last = local_terms(
-            keyrow, per_head(v_buf), cum_row, cum_col, str_row, str_col
-        )
+        cum_col = jnp.stack([cumul_turned[:, h : h + 1] for h in heads])
+        str_col = jnp.stack([strength_turned[:, h : h + 1] for h in heads])
+        keyrow, value = (
+            jnp.stack([buf[:, h * N : (h + 1) * N] for h in heads]) for buf in (k_buf, v_buf)
+        )
+        for_key, for_value, ratio, tail, last = local_solve(
+            keyrow, cum_row, cum_col, str_row, str_col
+        )
+        both, ends = local_ends(keyrow, value, for_key, for_value, tail)
         kept.append((heads, keyrow, ratio, both, cum_col))
-        head_send[start : start + BATCH, N + GROWS :, :] = (-ends[:, :, :N]).astype(BF16)
-        head_send[start : start + BATCH, :N, :] = ends[:, :, N:].astype(BF16)
+        part = slice(start, start + BATCH)
+        head_send[part, N + GROWS :, :] = (-ends[:, :, :N]).astype(BF16)
+        head_send[part, :N, :] = ends[:, :, N:].astype(BF16)
         for n, h in enumerate(heads):
             head_send[h, N : N + GROWS, :] = decay_rows(jnp.broadcast_to(last[n], (GROWS, N)))
 
@@ -305,22 +347,23 @@
     loads[4].wait()
     for heads, keyrow, ratio, both, cum_col in kept:
         query = jnp.stack([q_buf[:, h * N : (h + 1) * N] for h in heads])
-        reach, local = local_reads(query, keyrow, ratio, both, cum_col)
-        reach_buf[heads.start : heads.stop] = reach
-        local_buf[heads.start : heads.stop] = local
+        part = slice(heads.start, heads.stop)
+        reach_buf[part], local_buf[part] = local_reads(query, keyrow, ratio, both, cum_col)
 
     @pl.when(owner)
     def _():
         head_recv[mine] = head_send[own_head]
-        runs = [None, None]
-        for i in range(ROW):
-            for n in range(2):
-                at = n * ROW + i
+        runs = [None] * QUARTERS
+        for i in range(QUARTER):
+            for n in range(QUARTERS):
+                at = n * QUARTER + i
 
                 @pl.when(mine != at)
                 def _():
                     head_copy(0, at).wait_recv()
 
+            for n in range(QUARTERS):
+                at = n * QUARTER + i
                 step = read_message(head_recv, at)
                 if i == 0:
                     pre_g[at] = jnp.ones((8, N), F32)
@@ -333,15 +376,11 @@
                     pre_d[pl.ds(at * N, N), :] = run_d.astype(BF16)
                     pre_j[at] = run_j
                     runs[n] = advance(runs[n], step)
-        (first_g, first_d, first_j), (second_g, second_d, second_j) = runs
-        prod = dot_both(second_d, jnp.concatenate([first_d, first_j], axis=1))
-        total_buf[group, :N, :] = (second_g * first_j + second_j + prod[:, N:]).astype(BF16)
-        total_buf[group, N : N + GROWS, :] = decay_rows(
-            jnp.broadcast_to(first_g * second_g, (GROWS, N))
-        )
-        total_buf[group, N + GROWS :, :] = (
-            second_g * first_d + first_g * second_d + prod[:, :N]
-        ).astype(BF16)
+        first_half = join(runs[0], runs[1])
+        total_g, total_d, total_j = join(first_half, join(runs[2], runs[3]))
+        total_buf[group, :N, :] = total_j.astype(BF16)
+        total_buf[group, N : N + GROWS, :] = decay_rows(jnp.broadcast_to(total_g, (GROWS, N)))
+        total_buf[group, N + GROWS :, :] = total_d.astype(BF16)
 
         for source in range(GROUPS - 1):
 
@@ -349,6 +388,23 @@
             def _():
                 for target in range(source + 1, GROUPS):
                     total_copy(source, target).start()
+
+        befores = (runs[0], first_half, join(first_half, runs[2]))
+        for n, (before_g, before_d, before_j) in enumerate(befores, 1):
+            prod = dot_right(
+                pre_d[n * QUARTER * N : (n + 1) * QUARTER * N, :],
+                jnp.concatenate([before_d, before_j], axis=1),
+            )
+            for i in range(QUARTER):
+                at = n * QUARTER + i
+                lines = slice(i * N, (i + 1) * N)
+                gain = pre_g[at, :1, :]
+                own_d = pre_d[at * N : (at + 1) * N, :].astype(F32)
+                pre_j[at] = gain * before_j + pre_j[at] + prod[lines, N:]
+                pre_d[at * N : (at + 1) * N, :] = (
+                    gain * before_d + before_g * own_d + prod[lines, :N]
+                ).astype(BF16)
+                pre_g[at] = jnp.broadcast_to(gain * before_g, (8, N))
 
         state_buf[...] = jnp.zeros((N, N), F32)
         for source in range(GROUPS - 1):
@@ -366,16 +422,15 @@
                     )
 
         state = state_buf[...]
-        for n in range(2):
-            starts = dot(pre_d[n * ROW * N : (n + 1) * ROW * N, :], state)
-            for i in range(ROW):
-                at = n * ROW + i
-                moved = pre_g[at, :1, :] * state + starts[i * N : (i + 1) * N] + pre_j[at]
-                state_send[at] = moved.astype(BF16)
-            state = first_g * state + dot_left(first_d, state) + first_j
-        for peer in peers:
-            state_copy(peer).start()
-        state_recv[own_head] = state_send[mine]
+        for step in FARTHEST + (0,):
+            at = lax.rem(mine + step, GROUP)
+            moved = dot(pre_d[pl.ds(pl.multiple_of(at * N, N), N), :], state)
+            moved = moved + pre_g[at, :1, :] * state + pre_j[at]
+            state_send[at] = moved.astype(BF16)
+            if step:
+                state_copy(at).start()
+            else:
+                state_recv[own_head] = moved.astype(BF16)
 
     loads[5].wait()
     loads[6].wait()
@@ -504,20 +559,25 @@
             dma((CHUNKS, FANS)),
         ],
         compiler_params=pltpu.CompilerParams(
-            collective_id=0, has_side_effects=True, vmem_limit_bytes=64 * 1024 * 1024
+            collective_id=0, has_side_effects=True, vmem_limit_bytes=48 * 1024 * 1024
         ),
         cost_estimate=pl.CostEstimate(
             flops=2_000_000_000, bytes_accessed=6_000_000, transcendentals=500_000
         ),
     )(
-        query_vectors,
-        key_vectors,
-        value_vectors,
-        log_decay,
-        write_strength,
-        output_gate,
-        norm_gain.reshape(1, N),
-        out_proj,
+        *(
+            pltpu.with_memory_space_constraint(array, pltpu.HBM)
+            for array in (
+                query_vectors,
+                key_vectors,
+                value_vectors,
+                log_decay,
+                write_strength,
+                output_gate,
+                norm_gain.reshape(1, N),
+                out_proj,
+            )
+        )
     )
 
 

time: 43.1 us -> 39.2 us (0.910)
  Pallas kernels: 41 us -> 38.4 us
  local copies, waits for them, and re-layouts: 1.58 us -> 0.66 us
    pallas_call x1, Pallas kernels: 41 us -> 38.4 us  [on_device(): pl.pallas_call(kernel, out_shape=jax.ShapeDtypeStruct((rows // FANS, widt...]
    unnamed x1, local copies, waits for them, and re-layouts: 1.58 us -> 0.66 us
where the time goes in v3:
time: 39.2 us; the launch traced here: 39.1 us
  Pallas kernels  38.4 us (98%)
  local copies, waits for them, and re-layouts  0.66 us (2%)
    pallas_call x1, Pallas kernels, on_device(): pl.pallas_call(kernel, out_shape=jax.ShapeDtypeStruct((rows // FANS, widt...  38.4 us

profile of v3, /device:TPU:224, one launch (start us, length us, event | category | flops | bytes accessed | tf_op | source)
XLA Modules:
  0.0 39.1 jit_solution(11215887727635020305)
XLA Ops:
  0.0 38.4 %shard_map.82 = bf16[32,2304]{1,0:T(8,128)(2,1)S(1)} custom-call(bf16[128,1024]{1,0:T(8,128)(2,1)} %q_any.1, bf16[128,1024]{1,0:T(8,128)(2,1)} %k_any.1, bf16[128,1024]{1,0:T(8,128)(2,1)} %v_any.1, f32[8,128]{1,0:T(8,128)} %decay_any.1, f32[8,128]{1,0:T(8,128)} %strength_any.1, bf16[128,1024]{1,0:T(8,128)(2,1)} %gate_any.1, f32[1,128]{1,0:T(1,128)} %bitcast.1, ...), custom_call_target="tpu_custom_call" | custom-call | flops 2000000000 | bytes 6000000 | tf_op jit(solution)/shard_map/pallas_call | solution.py:523
  38.4 0.7 %copy.10 = bf16[32,2304]{1,0:T(8,128)(2,1)} copy(bf16[32,2304]{1,0:T(8,128)(2,1)S(1)} %shard_map.82) | data formatting | bytes 294912

commit v4 on v3

--- a/solution.py
+++ b/solution.py
@@ -9,22 +9,21 @@
 F32 = jnp.float32
 BF16 = jnp.bfloat16
 
-ROW = 8
 GROUP = 16
 GROUPS = 4
-QUARTERS = 4
-QUARTER = GROUP // QUARTERS
+CHIPS = GROUP // 2
+SIDE = 4
+HALVES = 2
+HALF = CHIPS // HALVES
 FANS = 4
 HEADS = 8
-BATCH = 8
+SHARE = HEADS // 2
 N = 128
 GROWS = 16
 MSG = GROWS + 2 * N
 CHUNKS = 3
-OWNERS = tuple(ROW * ((h % 4 + h // 4 + 1) % 2) + 2 * (h % 4) for h in range(HEADS))
 EPS = 1e-06
-
-FARTHEST = (4, 12, 5, 13, 3, 11, 2, 10, 6, 14, 7, 15, 1, 9, 8)
+FARTHEST = (2, 6, 1, 3, 5, 7, 4)
 
 
 def bdot(left, right, dims):
@@ -155,7 +154,7 @@
 
 
 def decay_rows(gain):
-    place = lax.broadcasted_iota(jnp.int32, (GROWS, N), 0)
+    place = lax.broadcasted_iota(jnp.int32, gain.shape, gain.ndim - 2)
     high = gain.astype(BF16).astype(F32)
     middle = (gain - high).astype(BF16).astype(F32)
     low = gain - high - middle
@@ -163,9 +162,9 @@
     return rows.astype(BF16)
 
 
-def read_message(buffer, index):
-    gain = jnp.sum(buffer[index, N : N + GROWS, :].astype(F32), axis=0, keepdims=True)
-    return gain, buffer[index, N + GROWS :, :], buffer[index, :N, :]
+def read_message(message):
+    gain = jnp.sum(message[..., N : N + GROWS, :].astype(F32), axis=-2, keepdims=True)
+    return gain, message[..., N + GROWS :, :], message[..., :N, :]
 
 
 def advance(run, step):
@@ -208,8 +207,9 @@
     gate_buf,
     gain_buf,
     proj_buf,
-    head_send,
-    head_recv,
+    terms,
+    chip_send,
+    chip_recv,
     pre_d,
     pre_j,
     pre_g,
@@ -223,8 +223,10 @@
     part_buf,
     part_recv,
     load_sem,
-    hs_sem,
-    hr_sem,
+    xs_sem,
+    xr_sem,
+    cs_sem,
+    cr_sem,
     ts_sem,
     tr_sem,
     ss_sem,
@@ -237,9 +239,13 @@
     group = place // GROUP
     mine = lax.rem(place, GROUP)
     base = group * GROUP
-    chip = lax.rem(mine, ROW) // 2
-    owner = lax.rem(mine, 2) == 0
-    own_head = chip + 4 * (1 - lax.rem(mine // ROW + chip, 2))
+    core = lax.rem(mine, 2)
+    chip = mine // 2
+    side = lax.rem(chip, SIDE)
+    partner = place + 1 - 2 * core
+    first_head = core * SHARE
+    owner = chip // SIDE == lax.rem(side + core + 1, 2)
+    own_head = first_head + side
     peers = [lax.rem(mine + step, GROUP) for step in range(1, GROUP)]
     fan_peers = [lax.rem(fan + step, FANS) for step in (2, 1, 3)]
 
@@ -278,13 +284,20 @@
             device_id_type=MESH,
         )
 
-    def head_copy(h, sender):
+    def pair_copy(half, sender):
+        part = terms.at[sender, pl.ds(half * SHARE, SHARE)]
+        return remote(part, part, xs_sem.at[half], xr_sem.at[half], (partner, fan))
+
+    def owner_chip(n):
+        return SIDE * lax.rem(n + core + 1, 2) + n
+
+    def chip_copy(n, sender):
         return remote(
-            head_send.at[h],
-            head_recv.at[sender],
-            hs_sem.at[h],
-            hr_sem.at[sender],
-            (base + OWNERS[h], fan),
+            chip_send.at[n],
+            chip_recv.at[sender],
+            cs_sem.at[n],
+            cr_sem.at[sender],
+            (base + 2 * owner_chip(n) + core, fan),
         )
 
     def total_copy(source, target):
@@ -297,16 +310,20 @@
             (target * GROUP + mine, fan),
         )
 
-    def state_copy(peer):
+    def state_copy(at):
         return remote(
-            state_send.at[peer],
+            state_send.at[at],
             state_recv.at[own_head],
-            ss_sem.at[peer],
+            ss_sem.at[at],
             sr_sem.at[own_head],
-            (base + peer, fan),
-        )
-
-    for load in loads[:4]:
+            (base + 2 * at + core, fan),
+        )
+
+    def share_copy(half):
+        part = state_recv.at[pl.ds(half * SHARE, SHARE)]
+        return remote(part, part, xs_sem.at[2], xr_sem.at[2], (partner, fan))
+
+    for load in loads[:5]:
         load.wait()
     row, col = places()
     below = mask(row[0] >= col[0])
@@ -315,56 +332,77 @@
     cumul_turned = sum(dot_turned(below, third) for third in decays)
     strength = strength_buf[...]
     strength_turned = sum(dot_turned(mask(row[0] == col[0]), third) for third in strengths)
-    kept = []
-    for start in range(0, HEADS, BATCH):
-        heads = range(start, start + BATCH)
-        cum_row = jnp.stack([cumul[h : h + 1, :] for h in heads])
-        str_row = jnp.stack([strength[h : h + 1, :] for h in heads])
-        cum_col = jnp.stack([cumul_turned[:, h : h + 1] for h in heads])
-        str_col = jnp.stack([strength_turned[:, h : h + 1] for h in heads])
-        keyrow, value = (
-            jnp.stack([buf[:, h * N : (h + 1) * N] for h in heads]) for buf in (k_buf, v_buf)
-        )
-        for_key, for_value, ratio, tail, last = local_solve(
-            keyrow, cum_row, cum_col, str_row, str_col
-        )
-        both, ends = local_ends(keyrow, value, for_key, for_value, tail)
-        kept.append((heads, keyrow, ratio, both, cum_col))
-        part = slice(start, start + BATCH)
-        head_send[part, N + GROWS :, :] = (-ends[:, :, :N]).astype(BF16)
-        head_send[part, :N, :] = ends[:, :, N:].astype(BF16)
-        for n, h in enumerate(heads):
-            head_send[h, N : N + GROWS, :] = decay_rows(jnp.broadcast_to(last[n], (GROWS, N)))
-
-        if start == 0:
-            pl.semaphore_wait(barrier, len(greeted))
-        for h in heads:
-
-            @pl.when(mine != OWNERS[h])
-            def _():
-                head_copy(h, mine).start()
-
-    loads[4].wait()
-    for heads, keyrow, ratio, both, cum_col in kept:
-        query = jnp.stack([q_buf[:, h * N : (h + 1) * N] for h in heads])
-        part = slice(heads.start, heads.stop)
-        reach_buf[part], local_buf[part] = local_reads(query, keyrow, ratio, both, cum_col)
+    heads = range(HEADS)
+    cum_row = jnp.stack([cumul[h : h + 1, :] for h in heads])
+    str_row = jnp.stack([strength[h : h + 1, :] for h in heads])
+    cum_col = jnp.stack([cumul_turned[:, h : h + 1] for h in heads])
+    str_col = jnp.stack([strength_turned[:, h : h + 1] for h in heads])
+    query, keyrow, value = (
+        jnp.stack([buf[:, h * N : (h + 1) * N] for h in heads]) for buf in (q_buf, k_buf, v_buf)
+    )
+    for_key, for_value, ratio, tail, last = local_solve(keyrow, cum_row, cum_col, str_row, str_col)
+    both, ends = local_ends(keyrow, value, for_key, for_value, tail)
+    own = terms.at[core]
+    own[:, :N, :] = ends[:, :, N:].astype(BF16)
+    own[:, N : N + GROWS, :] = decay_rows(jnp.broadcast_to(last, (HEADS, GROWS, N)))
+    own[:, N + GROWS :, :] = (-ends[:, :, :N]).astype(BF16)
+
+    pl.semaphore_wait(barrier, len(greeted))
+    pair_copy(1 - core, core).start()
+
+    @pl.when(core == 0)
+    def _():
+        pair_copy(0, core).start()
+
+    pair_copy(core, 1 - core).wait_recv()
+    share = pl.ds(first_head, SHARE)
+    first_g, first_d, first_j = read_message(terms[0, share])
+    second_g, second_d, second_j = read_message(terms[1, share])
+    prod = bdot(second_d, jnp.concatenate([first_d, first_j], axis=2), NN)
+    first_d, first_j, second_d, second_j = (
+        x.astype(F32) for x in (first_d, first_j, second_d, second_j)
+    )
+    chip_send[:, :N, :] = (second_g * first_j + second_j + prod[:, :, N:]).astype(BF16)
+    chip_send[:, N : N + GROWS, :] = decay_rows(
+        jnp.broadcast_to(first_g * second_g, (SHARE, GROWS, N))
+    )
+    chip_send[:, N + GROWS :, :] = (
+        second_g * first_d + first_g * second_d + prod[:, :, :N]
+    ).astype(BF16)
+
+    for n in range(SHARE):
+
+        @pl.when(chip != owner_chip(n))
+        def _():
+            chip_copy(n, chip).start()
+
+    reach, local = local_reads(query, keyrow, ratio, both, cum_col)
+    reach_buf[...] = reach
+    local_buf[...] = local
+
+    @pl.when(core == 1)
+    def _():
+        pair_copy(0, 0).wait_recv()
+        before_g, before_d, before_j = read_message(terms[0])
+        prod = bdot_left(reach_buf[...], jnp.concatenate([before_d, before_j], axis=2))
+        reach_buf[...] = before_g * reach_buf[...] + prod[:, :, :N]
+        local_buf[...] = local_buf[...] + prod[:, :, N:]
 
     @pl.when(owner)
     def _():
-        head_recv[mine] = head_send[own_head]
-        runs = [None] * QUARTERS
-        for i in range(QUARTER):
-            for n in range(QUARTERS):
-                at = n * QUARTER + i
-
-                @pl.when(mine != at)
+        chip_recv[chip] = chip_send[side]
+        runs = [None] * HALVES
+        for i in range(HALF):
+            for n in range(HALVES):
+                at = n * HALF + i
+
+                @pl.when(chip != at)
                 def _():
-                    head_copy(0, at).wait_recv()
-
-            for n in range(QUARTERS):
-                at = n * QUARTER + i
-                step = read_message(head_recv, at)
+                    chip_copy(0, at).wait_recv()
+
+            for n in range(HALVES):
+                at = n * HALF + i
+                step = read_message(chip_recv[at])
                 if i == 0:
                     pre_g[at] = jnp.ones((8, N), F32)
                     pre_d[pl.ds(at * N, N), :] = jnp.zeros((N, N), BF16)
@@ -376,8 +414,7 @@
                     pre_d[pl.ds(at * N, N), :] = run_d.astype(BF16)
                     pre_j[at] = run_j
                     runs[n] = advance(runs[n], step)
-        first_half = join(runs[0], runs[1])
-        total_g, total_d, total_j = join(first_half, join(runs[2], runs[3]))
+        total_g, total_d, total_j = join(runs[0], runs[1])
         total_buf[group, :N, :] = total_j.astype(BF16)
         total_buf[group, N : N + GROWS, :] = decay_rows(jnp.broadcast_to(total_g, (GROWS, N)))
         total_buf[group, N + GROWS :, :] = total_d.astype(BF16)
@@ -389,22 +426,18 @@
                 for target in range(source + 1, GROUPS):
                     total_copy(source, target).start()
 
-        befores = (runs[0], first_half, join(first_half, runs[2]))
-        for n, (before_g, before_d, before_j) in enumerate(befores, 1):
-            prod = dot_right(
-                pre_d[n * QUARTER * N : (n + 1) * QUARTER * N, :],
-                jnp.concatenate([before_d, before_j], axis=1),
-            )
-            for i in range(QUARTER):
-                at = n * QUARTER + i
-                lines = slice(i * N, (i + 1) * N)
-                gain = pre_g[at, :1, :]
-                own_d = pre_d[at * N : (at + 1) * N, :].astype(F32)
-                pre_j[at] = gain * before_j + pre_j[at] + prod[lines, N:]
-                pre_d[at * N : (at + 1) * N, :] = (
-                    gain * before_d + before_g * own_d + prod[lines, :N]
-                ).astype(BF16)
-                pre_g[at] = jnp.broadcast_to(gain * before_g, (8, N))
+        before_g, before_d, before_j = runs[0]
+        prod = dot_right(pre_d[HALF * N :, :], jnp.concatenate([before_d, before_j], axis=1))
+        for i in range(HALF):
+            at = HALF + i
+            lines = slice(i * N, (i + 1) * N)
+            gain = pre_g[at, :1, :]
+            own_d = pre_d[at * N : (at + 1) * N, :].astype(F32)
+            pre_j[at] = gain * before_j + pre_j[at] + prod[lines, N:]
+            pre_d[at * N : (at + 1) * N, :] = (
+                gain * before_d + before_g * own_d + prod[lines, :N]
+            ).astype(BF16)
+            pre_g[at] = jnp.broadcast_to(gain * before_g, (8, N))
 
         state_buf[...] = jnp.zeros((N, N), F32)
         for source in range(GROUPS - 1):
@@ -415,7 +448,7 @@
                 if source == 0:
                     state_buf[...] = total_buf[0, :N, :].astype(F32)
                 else:
-                    gain, step_d, step_j = read_message(total_buf, source)
+                    gain, step_d, step_j = read_message(total_buf[source])
                     state = state_buf[...]
                     state_buf[...] = (
                         gain * state + dot_right(step_d, state) + step_j.astype(F32)
@@ -423,7 +456,7 @@
 
         state = state_buf[...]
         for step in FARTHEST + (0,):
-            at = lax.rem(mine + step, GROUP)
+            at = lax.rem(chip + step, CHIPS)
             moved = dot(pre_d[pl.ds(pl.multiple_of(at * N, N), N), :], state)
             moved = moved + pre_g[at, :1, :] * state + pre_j[at]
             state_send[at] = moved.astype(BF16)
@@ -435,18 +468,21 @@
     loads[5].wait()
     loads[6].wait()
     gating = jax.nn.sigmoid(gate_buf[...].astype(F32)) * jnp.tile(gain_buf[...], (1, HEADS))
-    for h in range(HEADS):
-
-        @pl.when(mine != OWNERS[h])
+    for n in range(SHARE):
+
+        @pl.when(chip != owner_chip(n))
         def _():
+            head = first_head + n
             remote(
-                state_send.at[h],
-                state_recv.at[h],
-                ss_sem.at[h],
-                sr_sem.at[h],
-                (base + OWNERS[h], fan),
+                state_send.at[n],
+                state_recv.at[head],
+                ss_sem.at[n],
+                sr_sem.at[head],
+                (base + 2 * owner_chip(n) + core, fan),
             ).wait_recv()
 
+    share_copy(core).start()
+    share_copy(1 - core).wait_recv()
     outputs = bdot_left(reach_buf[...], state_recv[...]) + local_buf[...]
     square = jnp.mean(outputs * outputs, axis=2, keepdims=True)
     outputs = outputs * lax.rsqrt(square + EPS)
@@ -484,11 +520,17 @@
             summed = summed + part_recv[c, n].astype(F32)
         out_ref[:, c * width : (c + 1) * width] = summed.astype(BF16)
 
-    for h in range(HEADS):
-
-        @pl.when(mine != OWNERS[h])
+    pair_copy(1 - core, core).wait_send()
+
+    @pl.when(core == 0)
+    def _():
+        pair_copy(0, core).wait_send()
+
+    for n in range(SHARE):
+
+        @pl.when(chip != owner_chip(n))
         def _():
-            head_copy(h, mine).wait_send()
+            chip_copy(n, chip).wait_send()
 
     @pl.when(owner)
     def _():
@@ -499,9 +541,10 @@
                 for target in range(source + 1, GROUPS):
                     total_copy(source, target).wait_send()
 
-        for peer in peers:
-            state_copy(peer).wait_send()
-
+        for step in FARTHEST:
+            state_copy(lax.rem(chip + step, CHIPS)).wait_send()
+
+    share_copy(core).wait_send()
     for c in range(CHUNKS):
         for n, peer in enumerate(fan_peers):
             part_copy(c, n, fan, peer).wait_send()
@@ -534,14 +577,15 @@
             pltpu.VMEM((rows, wide), BF16),
             pltpu.VMEM((1, N), F32),
             pltpu.VMEM((depth, width), BF16),
-            pltpu.VMEM((HEADS, MSG, N), BF16),
-            pltpu.VMEM((GROUP, MSG, N), BF16),
-            pltpu.VMEM((GROUP * N, N), BF16),
-            pltpu.VMEM((GROUP, N, N), F32),
-            pltpu.VMEM((GROUP, 8, N), F32),
+            pltpu.VMEM((2, HEADS, MSG, N), BF16),
+            pltpu.VMEM((SHARE, MSG, N), BF16),
+            pltpu.VMEM((CHIPS, MSG, N), BF16),
+            pltpu.VMEM((CHIPS * N, N), BF16),
+            pltpu.VMEM((CHIPS, N, N), F32),
+            pltpu.VMEM((CHIPS, 8, N), F32),
             pltpu.VMEM((GROUPS, MSG, N), BF16),
             pltpu.VMEM((N, N), F32),
-            pltpu.VMEM((GROUP, N, N), BF16),
+            pltpu.VMEM((CHIPS, N, N), BF16),
             pltpu.VMEM((HEADS, N, N), BF16),
             pltpu.VMEM((HEADS, N, N), F32),
             pltpu.VMEM((HEADS, N, N), F32),
@@ -549,11 +593,13 @@
             pltpu.VMEM((CHUNKS, rows, width // CHUNKS), BF16),
             pltpu.VMEM((CHUNKS, FANS, rows // FANS, width // CHUNKS), BF16),
             dma((8,)),
-            dma((HEADS,)),
-            dma((GROUP,)),
+            dma((3,)),
+            dma((3,)),
+            dma((SHARE,)),
+            dma((CHIPS,)),
             dma((GROUPS,)),
             dma((GROUPS,)),
-            dma((GROUP,)),
+            dma((CHIPS,)),
             dma((HEADS,)),
             dma((CHUNKS, FANS - 1)),
             dma((CHUNKS, FANS)),

time: 39.2 us -> 37.5 us (0.957)
  Pallas kernels: 38.4 us -> 36.5 us
    pallas_call x1, Pallas kernels: 38.4 us -> 36.5 us  [on_device(): pl.pallas_call(kernel, out_shape=jax.ShapeDtypeStruct((rows // FANS, widt...]
where the time goes in v4:
time: 37.5 us; the launch traced here: 37.1 us
  Pallas kernels  36.5 us (97%)
  local copies, waits for them, and re-layouts  0.66 us (2%)
    pallas_call x1, Pallas kernels, on_device(): pl.pallas_call(kernel, out_shape=jax.ShapeDtypeStruct((rows // FANS, widt...  36.5 us

profile of v4, /device:TPU:224, one launch (start us, length us, event | category | flops | bytes accessed | tf_op | source)
XLA Modules:
  0.0 37.1 jit_solution(5467595999531707986)
XLA Ops:
  0.0 36.5 %shard_map.82 = bf16[32,2304]{1,0:T(8,128)(2,1)S(1)} custom-call(bf16[128,1024]{1,0:T(8,128)(2,1)} %q_any.1, bf16[128,1024]{1,0:T(8,128)(2,1)} %k_any.1, bf16[128,1024]{1,0:T(8,128)(2,1)} %v_any.1, f32[8,128]{1,0:T(8,128)} %decay_any.1, f32[8,128]{1,0:T(8,128)} %strength_any.1, bf16[128,1024]{1,0:T(8,128)(2,1)} %gate_any.1, f32[1,128]{1,0:T(1,128)} %bitcast.1, ...), custom_call_target="tpu_custom_call" | custom-call | flops 2000000000 | bytes 6000000 | tf_op jit(solution)/shard_map/pallas_call | solution.py:566
  36.5 0.7 %copy.10 = bf16[32,2304]{1,0:T(8,128)(2,1)} copy(bf16[32,2304]{1,0:T(8,128)(2,1)S(1)} %shard_map.82) | data formatting | bytes 294912

commit v5 on v4

--- a/solution.py
+++ b/solution.py
@@ -21,8 +21,11 @@
 N = 128
 GROWS = 16
 MSG = GROWS + 2 * N
-CHUNKS = 3
+CHUNKS = 6
 EPS = 1e-06
+OWNERS = tuple(
+    2 * (SIDE * ((h + h // SHARE + 1) % 2) + h % SHARE) + h // SHARE for h in range(HEADS)
+)
 FARTHEST = (2, 6, 1, 3, 5, 7, 4)
 
 
@@ -220,7 +223,9 @@
     reach_buf,
     local_buf,
     normed_buf,
+    share_buf,
     part_buf,
+    sum_buf,
     part_recv,
     load_sem,
     xs_sem,
@@ -247,7 +252,9 @@
     owner = chip // SIDE == lax.rem(side + core + 1, 2)
     own_head = first_head + side
     peers = [lax.rem(mine + step, GROUP) for step in range(1, GROUP)]
-    fan_peers = [lax.rem(fan + step, FANS) for step in (2, 1, 3)]
+    ahead = lax.rem(fan + 1 + 2 * core, FANS)
+    behind = lax.rem(fan + 3 - 2 * core, FANS)
+    opposite = lax.rem(fan + 2, FANS)
 
     loads = [
         pltpu.make_async_copy(source, target, load_sem.at[n])
@@ -270,7 +277,7 @@
     barrier = pltpu.get_barrier_semaphore()
     greeted = [(base + peer, fan) for peer in peers]
     greeted += [(lax.rem(place + step * GROUP, GROUPS * GROUP), fan) for step in range(1, GROUPS)]
-    greeted += [(place, peer) for peer in fan_peers]
+    greeted += [(place, ahead), (place, behind)]
     for device in greeted:
         pl.semaphore_signal(barrier, inc=1, device_id=device, device_id_type=MESH)
 
@@ -310,18 +317,20 @@
             (target * GROUP + mine, fan),
         )
 
-    def state_copy(at):
+    def state_copy(at, side_core):
         return remote(
             state_send.at[at],
             state_recv.at[own_head],
-            ss_sem.at[at],
+            ss_sem.at[at, side_core],
             sr_sem.at[own_head],
-            (base + 2 * at + core, fan),
-        )
-
-    def share_copy(half):
-        part = state_recv.at[pl.ds(half * SHARE, SHARE)]
-        return remote(part, part, xs_sem.at[2], xr_sem.at[2], (partner, fan))
+            (base + 2 * at + side_core, fan),
+        )
+
+    def state_copies():
+        for step in FARTHEST:
+            for side_core in range(2):
+                yield state_copy(lax.rem(chip + step, CHIPS), side_core)
+        yield state_copy(chip, 1 - core)
 
     for load in loads[:5]:
         load.wait()
@@ -455,34 +464,27 @@
                     )
 
         state = state_buf[...]
-        for step in FARTHEST + (0,):
-            at = lax.rem(chip + step, CHIPS)
-            moved = dot(pre_d[pl.ds(pl.multiple_of(at * N, N), N), :], state)
-            moved = moved + pre_g[at, :1, :] * state + pre_j[at]
-            state_send[at] = moved.astype(BF16)
-            if step:
-                state_copy(at).start()
-            else:
-                state_recv[own_head] = moved.astype(BF16)
+        moved = dot(pre_d[...], state).reshape(CHIPS, N, N) + pre_j[...]
+        state_send[...] = (moved + pre_g[:, :1, :] * state).astype(BF16)
+        for copy in state_copies():
+            copy.start()
+        state_recv[own_head] = state_send[chip]
 
     loads[5].wait()
     loads[6].wait()
     gating = jax.nn.sigmoid(gate_buf[...].astype(F32)) * jnp.tile(gain_buf[...], (1, HEADS))
-    for n in range(SHARE):
-
-        @pl.when(chip != owner_chip(n))
+    for h in range(HEADS):
+
+        @pl.when(mine != OWNERS[h])
         def _():
-            head = first_head + n
             remote(
-                state_send.at[n],
-                state_recv.at[head],
-                ss_sem.at[n],
-                sr_sem.at[head],
-                (base + 2 * owner_chip(n) + core, fan),
+                state_send.at[h],
+                state_recv.at[h],
+                ss_sem.at[h, 0],
+                sr_sem.at[h],
+                (base + OWNERS[h], fan),
             ).wait_recv()
 
-    share_copy(core).start()
-    share_copy(1 - core).wait_recv()
     outputs = bdot_left(reach_buf[...], state_recv[...]) + local_buf[...]
     square = jnp.mean(outputs * outputs, axis=2, keepdims=True)
     outputs = outputs * lax.rsqrt(square + EPS)
@@ -494,30 +496,40 @@
     rows = N // FANS
     width = proj_buf.shape[1] // CHUNKS
 
-    def part_copy(c, n, owner_fan, peer):
+    def lines(owner_fan):
+        return pl.ds(pl.multiple_of(owner_fan * rows, rows), rows)
+
+    def part_copy(c, kind):
+        source, to = (
+            (part_buf.at[c, lines(opposite)], ahead),
+            (part_buf.at[c, lines(behind)], behind),
+            (sum_buf.at[c], ahead),
+        )[kind]
         return remote(
-            part_buf.at[c, pl.ds(pl.multiple_of(peer * rows, rows), rows), :],
-            part_recv.at[c, owner_fan],
-            ps_sem.at[c, n],
-            pr_sem.at[c, owner_fan],
-            (place, peer),
+            source, part_recv.at[c, kind], ps_sem.at[c, kind], pr_sem.at[c, kind], (place, to)
         )
 
     for c in range(CHUNKS):
-        part_buf[c] = jnp.dot(
+        share = jnp.dot(
             normed_buf[...],
             proj_buf[:, c * width : (c + 1) * width],
             preferred_element_type=F32,
-        ).astype(BF16)
-        for n, peer in enumerate(fan_peers):
-            part_copy(c, n, fan, peer).start()
-        part_recv[c, fan] = part_buf[c, pl.ds(pl.multiple_of(fan * rows, rows), rows), :]
+        )
+        part_buf[c] = share.astype(BF16)
+        part_copy(c, 0).start()
+        share_buf[c] = share
     for c in range(CHUNKS):
-        for n, peer in enumerate(fan_peers):
-            part_copy(c, n, peer, peer).wait_recv()
-        summed = part_recv[c, 0].astype(F32)
-        for n in range(1, FANS):
-            summed = summed + part_recv[c, n].astype(F32)
+        part_copy(c, 1).start()
+    for c in range(CHUNKS):
+        part_copy(c, 0).wait_recv()
+        summed = share_buf[c, lines(ahead)] + part_recv[c, 0].astype(F32)
+        sum_buf[c] = summed.astype(BF16)
+        part_copy(c, 2).start()
+    for c in range(CHUNKS):
+        part_copy(c, 1).wait_recv()
+        part_copy(c, 2).wait_recv()
+        summed = share_buf[c, lines(fan)] + part_recv[c, 1].astype(F32)
+        summed = summed + part_recv[c, 2].astype(F32)
         out_ref[:, c * width : (c + 1) * width] = summed.astype(BF16)
 
     pair_copy(1 - core, core).wait_send()
@@ -541,13 +553,12 @@
                 for target in range(source + 1, GROUPS):
                     total_copy(source, target).wait_send()
 
-        for step in FARTHEST:
-            state_copy(lax.rem(chip + step, CHIPS)).wait_send()
-
-    share_copy(core).wait_send()
+        for copy in state_copies():
+            copy.wait_send()
+
     for c in range(CHUNKS):
-        for n, peer in enumerate(fan_peers):
-            part_copy(c, n, fan, peer).wait_send()
+        for kind in range(3):
+            part_copy(c, kind).wait_send()
 
 
 def on_device(
@@ -590,19 +601,21 @@
             pltpu.VMEM((HEADS, N, N), F32),
             pltpu.VMEM((HEADS, N, N), F32),
             pltpu.VMEM((rows, wide), BF16),
+            pltpu.VMEM((CHUNKS, rows, width // CHUNKS), F32),
             pltpu.VMEM((CHUNKS, rows, width // CHUNKS), BF16),
-            pltpu.VMEM((CHUNKS, FANS, rows // FANS, width // CHUNKS), BF16),
+            pltpu.VMEM((CHUNKS, rows // FANS, width // CHUNKS), BF16),
+            pltpu.VMEM((CHUNKS, 3, rows // FANS, width // CHUNKS), BF16),
             dma((8,)),
-            dma((3,)),
-            dma((3,)),
+            dma((2,)),
+            dma((2,)),
             dma((SHARE,)),
             dma((CHIPS,)),
             dma((GROUPS,)),
             dma((GROUPS,)),
-            dma((CHIPS,)),
+            dma((CHIPS, 2)),
             dma((HEADS,)),
-            dma((CHUNKS, FANS - 1)),
-            dma((CHUNKS, FANS)),
+            dma((CHUNKS, 3)),
+            dma((CHUNKS, 3)),
         ],
         compiler_params=pltpu.CompilerParams(
             collective_id=0, has_side_effects=True, vmem_limit_bytes=48 * 1024 * 1024

time: 37.5 us -> 36.5 us (0.973)
  Pallas kernels: 36.5 us -> 35.8 us
    pallas_call x1, Pallas kernels: 36.5 us -> 35.8 us  [on_device(): pl.pallas_call(kernel, out_shape=jax.ShapeDtypeStruct((rows // FANS, widt...]
where the time goes in v5:
time: 36.5 us
  Pallas kernels  35.8 us (98%)
  local copies, waits for them, and re-layouts  0.66 us (2%)
    pallas_call x1, Pallas kernels, on_device(): pl.pallas_call(kernel, out_shape=jax.ShapeDtypeStruct((rows // FANS, widt...  35.8 us

profile of v5, /device:TPU:224, one launch (start us, length us, event | category | flops | bytes accessed | tf_op | source)
XLA Modules:
  0.0 36.5 jit_solution(9677446486680458725)
XLA Ops:
  0.0 35.8 %shard_map.82 = bf16[32,2304]{1,0:T(8,128)(2,1)S(1)} custom-call(bf16[128,1024]{1,0:T(8,128)(2,1)} %q_any.1, bf16[128,1024]{1,0:T(8,128)(2,1)} %k_any.1, bf16[128,1024]{1,0:T(8,128)(2,1)} %v_any.1, f32[8,128]{1,0:T(8,128)} %decay_any.1, f32[8,128]{1,0:T(8,128)} %strength_any.1, bf16[128,1024]{1,0:T(8,128)(2,1)} %gate_any.1, f32[1,128]{1,0:T(1,128)} %bitcast.1, ...), custom_call_target="tpu_custom_call" | custom-call | flops 2000000000 | bytes 6000000 | tf_op jit(solution)/shard_map/pallas_call | solution.py:577
  35.8 0.7 %copy.10 = bf16[32,2304]{1,0:T(8,128)(2,1)} copy(bf16[32,2304]{1,0:T(8,128)(2,1)S(1)} %shard_map.82) | data formatting | bytes 294912

commit v6 on v5

--- a/solution.py
+++ b/solution.py
@@ -260,9 +260,9 @@
         pltpu.make_async_copy(source, target, load_sem.at[n])
         for n, (source, target) in enumerate(
             (
-                (k_any, k_buf),
                 (decay_any, decay_buf),
                 (strength_any, strength_buf),
+                (k_any, k_buf),
                 (v_any, v_buf),
                 (q_any, q_buf),
                 (gate_any, gate_buf),
@@ -332,7 +332,7 @@
                 yield state_copy(lax.rem(chip + step, CHIPS), side_core)
         yield state_copy(chip, 1 - core)
 
-    for load in loads[:5]:
+    for load in loads[:3]:
         load.wait()
     row, col = places()
     below = mask(row[0] >= col[0])
@@ -346,11 +346,14 @@
     str_row = jnp.stack([strength[h : h + 1, :] for h in heads])
     cum_col = jnp.stack([cumul_turned[:, h : h + 1] for h in heads])
     str_col = jnp.stack([strength_turned[:, h : h + 1] for h in heads])
-    query, keyrow, value = (
-        jnp.stack([buf[:, h * N : (h + 1) * N] for h in heads]) for buf in (q_buf, k_buf, v_buf)
-    )
+
+    def per_head(buf):
+        return jnp.stack([buf[:, h * N : (h + 1) * N] for h in heads])
+
+    keyrow = per_head(k_buf)
     for_key, for_value, ratio, tail, last = local_solve(keyrow, cum_row, cum_col, str_row, str_col)
-    both, ends = local_ends(keyrow, value, for_key, for_value, tail)
+    loads[3].wait()
+    both, ends = local_ends(keyrow, per_head(v_buf), for_key, for_value, tail)
     own = terms.at[core]
     own[:, :N, :] = ends[:, :, N:].astype(BF16)
     own[:, N : N + GROWS, :] = decay_rows(jnp.broadcast_to(last, (HEADS, GROWS, N)))
@@ -385,7 +388,8 @@
         def _():
             chip_copy(n, chip).start()
 
-    reach, local = local_reads(query, keyrow, ratio, both, cum_col)
+    loads[4].wait()
+    reach, local = local_reads(per_head(q_buf), keyrow, ratio, both, cum_col)
     reach_buf[...] = reach
     local_buf[...] = local
 
@@ -432,7 +436,7 @@
 
             @pl.when(group == source)
             def _():
-                for target in range(source + 1, GROUPS):
+                for target in reversed(range(source + 1, GROUPS)):
                     total_copy(source, target).start()
 
         before_g, before_d, before_j = runs[0]

time: 36.5 us -> 36 us (0.986)
  Pallas kernels: 35.8 us -> 35.2 us
    pallas_call x1, Pallas kernels: 35.8 us -> 35.2 us  [on_device(): pl.pallas_call(kernel, out_shape=jax.ShapeDtypeStruct((rows // FANS, widt...]
where the time goes in v6:
time: 36 us; the launch traced here: 35.9 us
  Pallas kernels  35.2 us (98%)
  local copies, waits for them, and re-layouts  0.66 us (2%)
    pallas_call x1, Pallas kernels, on_device(): pl.pallas_call(kernel, out_shape=jax.ShapeDtypeStruct((rows // FANS, widt...  35.2 us

profile of v6, /device:TPU:224, one launch (start us, length us, event | category | flops | bytes accessed | tf_op | source)
XLA Modules:
  0.0 35.9 jit_solution(17821392186858152218)
XLA Ops:
  0.0 35.2 %shard_map.82 = bf16[32,2304]{1,0:T(8,128)(2,1)S(1)} custom-call(bf16[128,1024]{1,0:T(8,128)(2,1)} %q_any.1, bf16[128,1024]{1,0:T(8,128)(2,1)} %k_any.1, bf16[128,1024]{1,0:T(8,128)(2,1)} %v_any.1, f32[8,128]{1,0:T(8,128)} %decay_any.1, f32[8,128]{1,0:T(8,128)} %strength_any.1, bf16[128,1024]{1,0:T(8,128)(2,1)} %gate_any.1, f32[1,128]{1,0:T(1,128)} %bitcast.1, ...), custom_call_target="tpu_custom_call" | custom-call | flops 2000000000 | bytes 6000000 | tf_op jit(solution)/shard_map/pallas_call | solution.py:581
  35.2 0.7 %copy.10 = bf16[32,2304]{1,0:T(8,128)(2,1)} copy(bf16[32,2304]{1,0:T(8,128)(2,1)S(1)} %shard_map.82) | data formatting | bytes 294912

commit v7 on v6

--- a/solution.py
+++ b/solution.py
@@ -382,11 +382,12 @@
         second_g * first_d + first_g * second_d + prod[:, :, :N]
     ).astype(BF16)
 
-    for n in range(SHARE):
-
-        @pl.when(chip != owner_chip(n))
-        def _():
-            chip_copy(n, chip).start()
+    for step in (2, 1, 3):
+        chip_copy(lax.rem(side + step, SIDE), chip).start()
+
+    @pl.when(jnp.logical_not(owner))
+    def _():
+        chip_copy(side, chip).start()
 
     loads[4].wait()
     reach, local = local_reads(per_head(q_buf), keyrow, ratio, both, cum_col)

time: 36 us -> 35.7 us (level)
  Pallas kernels: 35.2 us -> 34.7 us
    pallas_call x1, Pallas kernels: 35.2 us -> 34.7 us  [on_device(): pl.pallas_call(kernel, out_shape=jax.ShapeDtypeStruct((rows // FANS, widt...]
where the time goes in v7:
time: 35.7 us; the launch traced here: 35.3 us
  Pallas kernels  34.7 us (97%)
  local copies, waits for them, and re-layouts  0.66 us (2%)
    pallas_call x1, Pallas kernels, on_device(): pl.pallas_call(kernel, out_shape=jax.ShapeDtypeStruct((rows // FANS, widt...  34.7 us

profile of v7, /device:TPU:224, one launch (start us, length us, event | category | flops | bytes accessed | tf_op | source)
XLA Modules:
  0.0 35.3 jit_solution(4248734592555840906)
XLA Ops:
  0.0 34.7 %shard_map.82 = bf16[32,2304]{1,0:T(8,128)(2,1)S(1)} custom-call(bf16[128,1024]{1,0:T(8,128)(2,1)} %q_any.1, bf16[128,1024]{1,0:T(8,128)(2,1)} %k_any.1, bf16[128,1024]{1,0:T(8,128)(2,1)} %v_any.1, f32[8,128]{1,0:T(8,128)} %decay_any.1, f32[8,128]{1,0:T(8,128)} %strength_any.1, bf16[128,1024]{1,0:T(8,128)(2,1)} %gate_any.1, f32[1,128]{1,0:T(1,128)} %bitcast.1, ...), custom_call_target="tpu_custom_call" | custom-call | flops 2000000000 | bytes 6000000 | tf_op jit(solution)/shard_map/pallas_call | solution.py:582
  34.7 0.7 %copy.10 = bf16[32,2304]{1,0:T(8,128)(2,1)} copy(bf16[32,2304]{1,0:T(8,128)(2,1)S(1)} %shard_map.82) | data formatting | bytes 294912
